TPU v7x, 32 devices: a whole 2x2x4 slice. The times are simulated.
32 devices in a mesh: grp: 2 (over x), ep: 16 (over z, y, core).
Axes of the slice: x: 2, y: 2, z: 4, core: 2. Of those that a mesh axis runs over, the one named last changes fastest.
Arguments:
- resid: bfloat16 [2048, 2048], P('ep', 'grp'), may hold values from -6 to 6
- query: bfloat16 [2048, 2048], P('ep', 'grp'), may hold values from -6 to 6
- key_new: bfloat16 [2048, 2048], P('ep', 'grp'), may hold values from -6 to 6
- value_new: bfloat16 [2048, 2048], P('ep', 'grp'), may hold values from -6 to 6
- cache_kv: bfloat16 [2, 16384, 2048], P(None, 'ep', 'grp'), may hold values from -6 to 6
- cache_len: int32 [16], replicated, may hold values from 1 to 1024, 4096 in all
- w_out: bfloat16 [2048, 2048], P('grp'), may hold values from -0.125 to 0.125
- norm_gain: bfloat16 [2048], replicated, may hold values from 0.099609375 to 1.8984375
- w_router: bfloat16 [2048, 16], replicated, may hold values from -7 to 7
- routes: int32 [2048, 4], P('ep'), may hold values from 0 to 15, all different within a row; in each aligned block of 128 rows (0 to 127, 128 to 255, ...) at most 64 rows name the same one
- w_gate_up: bfloat16 [16, 2, 2048, 1408], P('ep', None, None, 'grp'), may hold values from -0.125 to 0.125
- w_down: bfloat16 [16, 1408, 2048], P('ep', 'grp'), may hold values from -0.15625 to 0.15625
Outputs:
- after_attention: bfloat16 [2048, 2048], P('ep', 'grp')
- expert_mix: bfloat16 [2048, 2048], P('ep', 'grp')
Inputs may be any that keep to these rules, and one draw needn't show every extreme that they name: `routes`: in each aligned block of 128 rows (one request's tokens), no expert is named by more than 64 of the pairs, and in every draw some expert is named by exactly 64. Request r's cache fills the first cache_len[r] rows of its slab, rows r * 1024 onward of cache_kv; the rest of the slab is unused; the lengths sum to 4096 and the longest is exactly 1024.
All inputs are finite; a program needn't handle non-finite values.
Results may differ from a plain program's by a relative error of at most 0.013.
Values may be sent and summed in bfloat16 or wider, within the bound.
A program may use at most 64 MiB of HBM per device.

v0:
```python
import jax
import jax.numpy as jnp
from jax import lax
from jax.sharding import PartitionSpec as P

D = 2048
HD = 128
TOP = 4


EPS = 1e-06
MASKED = -1e30


def expert_rows(arrived, w_gate_up, w_down):
    features = arrived.shape[-1]
    flat_rows = arrived.reshape(-1, features)
    gate_value = jnp.dot(flat_rows, w_gate_up[0, 0], preferred_element_type=jnp.float32)
    up_value = jnp.dot(flat_rows, w_gate_up[0, 1], preferred_element_type=jnp.float32)
    hidden = (jax.nn.silu(gate_value) * up_value).astype(jnp.bfloat16)
    partial_value = jnp.dot(hidden, w_down[0], preferred_element_type=jnp.float32).astype(
        jnp.bfloat16
    )
    return partial_value.reshape(arrived.shape)


def send_back(answered):
    return lax.all_to_all(answered, "ep", split_axis=0, concat_axis=0, tiled=True)


def body(
    resid,
    query,
    key_new,
    value_new,
    cache_kv,
    cache_len,
    w_out,
    norm_gain,
    w_router,
    routes,
    w_gate_up,
    w_down,
):
    tokens_here = query.shape[0]
    heads_here = query.shape[1] // HD
    experts_all = w_router.shape[1]
    column_width = resid.shape[1]
    group_index = lax.axis_index("grp")
    request = lax.axis_index("ep")
    capacity = max(2, 8 * tokens_here // lax.axis_size("ep"))
    score_scale = float(HD) ** (-0.5)
    column_start = group_index * column_width
    queries = query.reshape(tokens_here, heads_here, HD)
    new_keys = key_new.reshape(tokens_here, heads_here, HD)
    new_values = value_new.reshape(tokens_here, heads_here, HD)
    cache_rows = cache_kv.shape[1]
    cache_keys = cache_kv[0].reshape(cache_rows, heads_here, HD)
    cache_values = cache_kv[1].reshape(cache_rows, heads_here, HD)
    own_length = lax.dynamic_index_in_dim(cache_len, request, 0, keepdims=False)
    position = jnp.arange(tokens_here, dtype=jnp.int32)
    causal = (position[:, None] >= position[None, :])[:, None, :]
    new_scores = (
        jnp.einsum("qhd,khd->qhk", queries, new_keys, preferred_element_type=jnp.float32)
        * score_scale
    )
    new_scores = jnp.where(causal, new_scores, MASKED)
    live_rows = (jnp.arange(cache_rows, dtype=jnp.int32) < own_length)[None, None, :]
    old_scores = (
        jnp.einsum("qhd,khd->qhk", queries, cache_keys, preferred_element_type=jnp.float32)
        * score_scale
    )
    old_scores = jnp.where(live_rows, old_scores, MASKED)
    row_max = jnp.maximum(jnp.max(new_scores, axis=-1), jnp.max(old_scores, axis=-1))
    new_probs = jnp.exp(new_scores - row_max[..., None])
    old_probs = jnp.exp(old_scores - row_max[..., None])
    denominator = jnp.sum(new_probs, axis=-1) + jnp.sum(old_probs, axis=-1)
    weighted = jnp.einsum(
        "qhk,khd->qhd",
        new_probs.astype(jnp.bfloat16),
        new_values,
        preferred_element_type=jnp.float32,
    )
    weighted = weighted + jnp.einsum(
        "qhk,khd->qhd",
        old_probs.astype(jnp.bfloat16),
        cache_values,
        preferred_element_type=jnp.float32,
    )
    attended = (
        (weighted / denominator[..., None])
        .astype(jnp.bfloat16)
        .reshape(tokens_here, heads_here * HD)
    )
    projected = jnp.dot(attended, w_out, preferred_element_type=jnp.float32)
    attn_share = lax.psum_scatter(projected, "grp", scatter_dimension=1, tiled=True)
    after_cols = (resid.astype(jnp.float32) + attn_share).astype(jnp.bfloat16)
    after_wide = after_cols.astype(jnp.float32)
    squares = lax.psum(jnp.sum(after_wide * after_wide, axis=1), "grp")
    inverse = lax.rsqrt(squares / D + EPS)
    gain_cols = lax.dynamic_slice_in_dim(norm_gain, column_start, column_width, 0)
    normed_cols = (after_wide * inverse[:, None] * gain_cols.astype(jnp.float32)[None, :]).astype(
        jnp.bfloat16
    )
    router_cols = lax.dynamic_slice_in_dim(w_router, column_start, column_width, 0)
    logits = lax.psum(jnp.dot(normed_cols, router_cols, preferred_element_type=jnp.float32), "grp")
    normed_full = lax.all_gather(normed_cols, "grp", axis=1, tiled=True)
    route_hits = routes[:, :, None] == jnp.arange(experts_all, dtype=jnp.int32)[None, None, :]
    chosen = jnp.sum(jnp.where(route_hits, logits[:, None, :], 0.0), axis=-1)
    route_weight = jax.nn.softmax(chosen, axis=-1).astype(jnp.bfloat16)
    flat_hits = route_hits.reshape(tokens_here * TOP, experts_all).astype(jnp.int32)
    earlier = jnp.cumsum(flat_hits, axis=0) - flat_hits
    slot_index = jnp.sum(earlier * flat_hits, axis=1)
    slot_row = (routes.reshape(-1) * capacity + slot_index).reshape(tokens_here, TOP)
    slot_ids = jnp.arange(experts_all * capacity, dtype=jnp.int32)
    matches = slot_row[:, :, None] == slot_ids[None, None, :]
    selection = jnp.any(matches, axis=1).astype(jnp.bfloat16)
    combine = jnp.sum(
        jnp.where(matches, route_weight[:, :, None], jnp.zeros((), jnp.bfloat16)), axis=1
    )
    outgoing = jnp.einsum(
        "tj,td->jd", selection, normed_full, preferred_element_type=jnp.float32
    ).astype(jnp.bfloat16)
    outgoing = outgoing.reshape(experts_all, capacity, D)
    returned = send_back(
        expert_rows(
            lax.all_to_all(outgoing, "ep", split_axis=0, concat_axis=0, tiled=True),
            w_gate_up,
            w_down,
        )
    )
    mixed_part = jnp.dot(
        combine, returned.reshape(experts_all * capacity, D), preferred_element_type=jnp.float32
    )
    mixed_cols = lax.psum_scatter(mixed_part, "grp", scatter_dimension=1, tiled=True)
    return (after_cols, mixed_cols.astype(jnp.bfloat16))


def solution(mesh):
    return jax.shard_map(
        body,
        mesh=mesh,
        in_specs=(
            P("ep", "grp"),
            P("ep", "grp"),
            P("ep", "grp"),
            P("ep", "grp"),
            P(None, "ep", "grp"),
            P(),
            P("grp", None),
            P(),
            P(),
            P("ep", None),
            P("ep", None, None, "grp"),
            P("ep", "grp", None),
        ),
        out_specs=(P("ep", "grp"), P("ep", "grp")),
        check_vma=False,
    )
```

profile of v0, /device:TPU:0, one launch (start us, length us, event | category | flops | bytes accessed | tf_op | source)
XLA Modules:
  0.0 316.8 jit_solution(15092613477775903002)
XLA Ops:
  7.3 1.4 dynamic_slice.10
  10.4 4.6 %fusion.53 = (bf16[1,1024,1024]{2,1,0:T(8,128)(2,1)}, bf16[1,1024,1024]{2,1,0:T(8,128)(2,1)}) fusion(bf16[2,1024,1024]{2,1,0:T(8,128)(2,1)} %param.16), kind=kLoop, calls=%fused_computation.74 | loop fusion | bytes 8388608 | tf_op jit(solution)/shard_map/slice | solution.py:58
  15.1 4.0 %copy.72 = bf16[1,1024,1024]{1,2,0:T(8,128)(2,1)} copy(bf16[1,1024,1024]{2,1,0:T(8,128)(2,1)} %get-tuple-element.4) | data formatting | bytes 4194304
  19.1 3.9 %copy.62 = bf16[1,1024,1024]{1,2,0:T(8,128)(2,1)} copy(bf16[1,1024,1024]{2,1,0:T(8,128)(2,1)} %get-tuple-element.5) | data formatting | bytes 4194304 | tf_op jit(solution)/shard_map/slice | solution.py:59
  23.0 1.3 fusion.54
  24.3 3.0 bitcast_reduce_fusion
  28.3 1.6 fusion.10
  30.5 1.7 fusion.55
  32.6 1.2 reduce-window.6
  34.7 20.7 %reduce-scatter.3.cloned.1.call-done = f32[128,1024]{1,0:T(8,128)} async-done(((f32[128,2048]{1,0:T(8,128)}), f32[128,1024]{1,0:T(8,128)}) %reduce-scatter.3.cloned.1.call-update) | async-done | bytes 524304 | tf_op jit(solution)/shard_map/reduce_scatter | solution.py:96
  55.4 1.3 fusion.28
  56.7 4.9 %psum.14 = f32[128]{0:T(128)S(1)} all-reduce(f32[128]{0:T(128)S(1)} %get-tuple-element.2), channel_id=1, replica_groups=mesh['grp'=2,'ep'=16] {'grp'}, use_global_device_ids=true, to_apply=%region_9.10 | all-reduce | flops 128 | bytes 1024 | tf_op jit(solution)/shard_map/psum | solution.py:99
  61.8 7.6 %all_gather.3 = bf16[128,2048]{1,0:T(8,128)(2,1)S(1)} all-gather(bf16[128,1024]{1,0:T(8,128)(2,1)S(1)} %fusion.30), channel_id=1, replica_groups=mesh['grp'=2,'ep'=16] {'grp'}, dimensions={1}, use_global_device_ids=true | all-gather | bytes 786432 | tf_op jit(solution)/shard_map/all_gather | solution.py:107
  69.4 1.3 convolution_convert_fusion.1
  70.7 97.8 %all_to_all.10 = bf16[16,64,2048]{2,1,0:T(8,128)(2,1)S(1)} all-to-all(bf16[16,64,2048]{2,1,0:T(8,128)(2,1)S(1)} %bitcast.98), channel_id=1, replica_groups=mesh['grp'=2,'ep'=16] {'ep'}, dimensions={0} | all-to-all | bytes 8388608 | tf_op jit(solution)/shard_map/all_to_all | solution.py:127
  168.5 2.0 copy-done.2
  170.5 4.8 %fusion.4 = f32[1024,704]{0,1:T(8,128)} fusion(bf16[1024,2048]{1,0:T(8,128)(2,1)S(1)} %bitcast.101, bf16[1,2,2048,704]{2,3,1,0:T(8,128)(2,1)S(1)} %bitcast.107), kind=kOutput, calls=%fused_computation.9 | convolution fusion | flops 2952790016 | bytes 9961472 | tf_op jit(solution)/shard_map/dot_general | solution.py:19
  175.3 11.3 %convolution_convert_fusion = bf16[1024,2048]{1,0:T(8,128)(2,1)} fusion(bf16[1,704,2048]{2,1,0:T(8,128)(2,1)S(1)} %copy-done, f32[1024,704]{0,1:T(8,128)} %fusion.4, bf16[1024,2048]{1,0:T(8,128)(2,1)} %bitcast.102, bf16[1,2,2048,704]{2,3,1,0:T(8,128)(2,1)} %param.22), kind=kOutput, calls=%fused_computation.4 | convolution fusion | flops 5912002560 | bytes 17039360 | tf_op jit(solution)/shard_map/dot_general | solution.py:21
  186.6 5.5 %all-to-all-start.1 = ((bf16[16,64,2048]{2,1,0:T(8,128)(2,1)}), bf16[16,64,2048]{2,1,0:T(8,128)(2,1)}, u32[]{:S(2)}, u32[]{:S(2)}) async-start(bf16[16,64,2048]{2,1,0:T(8,128)(2,1)} %bitcast.100), calls=%async_computation.2 | async-start | bytes 8388608 | tf_op jit(solution)/shard_map/all_to_all | solution.py:28
  192.3 5.0 %psum.15 = f32[128,16]{0,1:T(8,128)S(1)} all-reduce(f32[128,16]{0,1:T(8,128)S(1)} %fusion.45), channel_id=1, replica_groups=mesh['grp'=2,'ep'=16] {'grp'}, use_global_device_ids=true, to_apply=%region_10.11 | all-reduce | flops 2048 | bytes 16384 | tf_op jit(solution)/shard_map/psum | solution.py:106
  197.7 72.1 %all-to-all-done.1 = bf16[16,64,2048]{2,1,0:T(8,128)(2,1)} async-done(((bf16[16,64,2048]{2,1,0:T(8,128)(2,1)}), bf16[16,64,2048]{2,1,0:T(8,128)(2,1)}, u32[]{:S(2)}, u32[]{:S(2)}) %all-to-all-start.1) | async-done | bytes 4194336 | tf_op jit(solution)/shard_map/all_to_all | solution.py:28
  269.8 3.9 %fusion.56 = f32[128,2048]{1,0:T(8,128)} fusion(bf16[128,1024]{1,0:T(8,128)(2,1)S(1)} %fusion.25, bf16[1024,2048]{1,0:T(8,128)(2,1)} %bitcast.15), kind=kOutput, calls=%fused_computation.77 | convolution fusion | flops 536870912 | bytes 5505024 | tf_op jit(solution)/shard_map/dot_general | solution.py:132
  273.7 34.5 %reduce-scatter.5.cloned.1.call-done = f32[128,1024]{1,0:T(8,128)} async-done(((f32[128,2048]{1,0:T(8,128)}), f32[128,1024]{1,0:T(8,128)}) %reduce-scatter.5.cloned.1.call-update) | async-done | bytes 524304 | tf_op jit(solution)/shard_map/reduce_scatter | solution.py:135
  308.2 1.8 convert_element_type.67
  (55 shorter events, 5.4 us)
Async XLA Ops:
  7.2 168.2 %copy-start = (bf16[1,704,2048]{2,1,0:T(8,128)(2,1)S(1)}, bf16[1,704,2048]{2,1,0:T(8,128)(2,1)}, u32[]{:S(2)}) copy-start(bf16[1,704,2048]{2,1,0:T(8,128)(2,1)} %param.23) | copy-start | bytes 8650756
  7.2 48.2 %reduce-scatter.3.cloned.1.call-start = ((), (), s32[]{:S(2)}) async-start(), calls=%async_computation.4 | async-start | bytes 1572864 | tf_op jit(solution)/shard_map/reduce_scatter | solution.py:96
  15.1 7.9 %copy-start.5 = (bf16[128,1024]{1,0:T(8,128)(2,1)S(1)}, bf16[128,1024]{1,0:T(8,128)(2,1)}, u32[]{:S(2)}) copy-start(bf16[128,1024]{1,0:T(8,128)(2,1)} %param.13) | copy-start | bytes 786436
  24.3 4.0 %copy-start.3 = (bf16[1,1024,1024]{1,2,0:T(8,128)(2,1)S(1)}, bf16[1,1024,1024]{1,2,0:T(8,128)(2,1)}, u32[]{:S(2)}) copy-start(bf16[1,1024,1024]{1,2,0:T(8,128)(2,1)} %copy.62) | copy-start | bytes 6291460
  28.3 2.2 copy-start.1
  30.0 2.2 copy-start.6
  30.0 4.3 %copy-start.8 = (bf16[2048]{0:T(1024)(128)(2,1)S(1)}, bf16[2048]{0:T(1024)(128)(2,1)}, u32[]{:S(2)}) copy-start(bf16[2048]{0:T(1024)(128)(2,1)} %param.19) | copy-start | bytes 12292
  56.7 14.0 %copy-start.4 = (bf16[128,1024]{1,0:T(8,128)(2,1)}, bf16[128,1024]{1,0:T(8,128)(2,1)S(1)}, u32[]{:S(2)}) copy-start(bf16[128,1024]{1,0:T(8,128)(2,1)S(1)} %get-tuple-element.3) | copy-start | bytes 786436
  69.4 101.1 %slice-start = ((s8[5767168]{0:T(1024)(128)(4,1)}), s8[4194304]{0:T(1024)(128)(4,1)S(1)}, s32[]{:S(2)}) async-start(s8[5767168]{0:T(1024)(128)(4,1)} %bitcast.106), calls=%async_computation.6 | async-start | bytes 8388608
  70.7 99.8 %slice-start.1 = ((s8[5767168]{0:T(1024)(128)(4,1)}), s8[1572864]{0:T(1024)(128)(4,1)S(1)}, s32[]{:S(2)}) async-start(s8[5767168]{0:T(1024)(128)(4,1)} %bitcast.106), calls=%async_computation.7 | async-start | bytes 3145728
  168.5 2.0 copy-start.2
  186.6 5.5 %copy-start.7 = (bf16[2048,16]{0,1:T(8,128)(2,1)S(1)}, bf16[2048,16]{0,1:T(8,128)(2,1)}, u32[]{:S(2)}) copy-start(bf16[2048,16]{0,1:T(8,128)(2,1)} %param.20) | copy-start | bytes 196612
  186.6 83.2 %all-to-all-start.1 = ((bf16[16,64,2048]{2,1,0:T(8,128)(2,1)}), bf16[16,64,2048]{2,1,0:T(8,128)(2,1)}, u32[]{:S(2)}, u32[]{:S(2)}) async-start(bf16[16,64,2048]{2,1,0:T(8,128)(2,1)} %bitcast.100), calls=%async_computation.2 | async-start | bytes 8388608 | tf_op jit(solution)/shard_map/all_to_all | solution.py:28
  192.1 116.1 %reduce-scatter.5.cloned.1.call-start = ((), (), s32[]{:S(2)}) async-start(), calls=%async_computation.5 | async-start | bytes 1572864 | tf_op jit(solution)/shard_map/reduce_scatter | solution.py:135
Sparse Core Ops, SparseCore 0:
  32.4 22.9 reduce-scatter.2
  273.8 34.3 reduce-scatter.4
where the time goes:
time: 317 us
  waiting for transfers between devices  127 us (40%)
  blocking collectives  115 us (36%)
  matrix products  29.4 us (9%)
  local copies, waits for them, and re-layouts  18 us (6%)
  between operations  14.3 us (5%)
  other arithmetic  6.94 us (2%)
  starting transfers between devices  5.56 us (2%)
    all_to_all x1, blocking collectives, body(): lax.all_to_all(outgoing, 'ep', split_axis=0, concat_axis=0, tiled=True)  97.8 us
    all_to_all x1, waiting for transfers between devices, send_back(): lax.all_to_all(answered, 'ep', split_axis=0, concat_axis=0, tiled=True)  72.1 us
    reduce_scatter x1, waiting for transfers between devices, body(): lax.psum_scatter(mixed_part, 'grp', scatter_dimension=1, tiled=True)  34.5 us
    reduce_scatter x1, waiting for transfers between devices, body(): lax.psum_scatter(projected, 'grp', scatter_dimension=1, tiled=True)  20.7 us
    dot_general x1, matrix products, expert_rows(): jnp.dot(hidden, w_down[0], preferred_element_type=jnp.float32)  11.3 us
    all_gather x1, blocking collectives, body(): normed_full = lax.all_gather(normed_cols, 'grp', axis=1, tiled=True)  7.59 us
  transfers between devices with their start and end apart: 3, of which 3 were waited for; matrix products, arithmetic and copies ran while one was open for 1% of the time, Pallas kernels for 0%

commit v1 on v0

--- a/solution.py
+++ b/solution.py
@@ -1,6 +1,8 @@
 import jax
 import jax.numpy as jnp
 from jax import lax
+from jax.experimental import pallas as pl
+from jax.experimental.pallas import tpu as pltpu
 from jax.sharding import PartitionSpec as P
 
 D = 2048
@@ -28,7 +30,7 @@
     return lax.all_to_all(answered, "ep", split_axis=0, concat_axis=0, tiled=True)
 
 
-def body(
+def wide_body(
     resid,
     query,
     key_new,
@@ -136,9 +138,415 @@
     return (after_cols, mixed_cols.astype(jnp.bfloat16))
 
 
+FIRST = 80
+BATCH = 4
+
+
+def exchange_kernel(
+    normed_ref,
+    slots_ref,
+    router_ref,
+    gate_up_hbm,
+    down_hbm,
+    out_ref,
+    tokens,
+    partial,
+    from_core,
+    from_x,
+    from_x_last,
+    from_y,
+    from_y_last,
+    from_z,
+    from_z_last,
+    gate_up,
+    down,
+    rows_in,
+    hidden,
+    combine,
+    weight_sem,
+    send_sem,
+    recv_sem,
+):
+    count = normed_ref.shape[0]
+    width = normed_ref.shape[1]
+    capacity = combine.shape[1]
+    experts = router_ref.shape[0]
+    here = lax.axis_index("grp")
+    there = 1 - here
+    place = lax.axis_index("ep")
+    core = lax.rem(place, 2)
+    y_at = lax.rem(lax.div(place, 2), 2)
+    z_low = lax.rem(lax.div(place, 4), 2)
+    z_high = lax.div(place, 8)
+
+    def moved(dz, dy, dc):
+        high = 1 - z_high if dz // 2 else z_high
+        low = 1 - z_low if dz % 2 else z_low
+        along_y = 1 - y_at if dy else y_at
+        on_core = 1 - core if dc else core
+        return ((high * 2 + low) * 2 + along_y) * 2 + on_core
+
+    by_x = (there, place)
+    by_y = (here, moved(0, 1, 0))
+    by_core = (here, moved(0, 0, 1))
+    by_z = [None] + [(here, moved(dz, 0, 0)) for dz in (1, 2, 3)]
+
+    weights = [
+        pltpu.make_async_copy(gate_up_hbm.at[0], gate_up, weight_sem.at[0]),
+        pltpu.make_async_copy(down_hbm.at[0], down, weight_sem.at[1]),
+    ]
+    for one in weights:
+        one.start()
+
+    barrier = pltpu.get_barrier_semaphore()
+    peers = [by_x, by_y, by_core] + by_z[1:]
+    for peer in peers:
+        pl.semaphore_signal(barrier, inc=1, device_id=peer, device_id_type=pl.DeviceIdType.MESH)
+
+    tokens[0, here] = normed_ref[...]
+    pl.semaphore_wait(barrier, len(peers))
+
+    first = pl.ds(0, FIRST)
+    last = pl.ds(FIRST, count - FIRST)
+    started = []
+
+    def send(source, target, peer):
+        index = len(started)
+        copy = pltpu.make_async_remote_copy(
+            src_ref=source,
+            dst_ref=target,
+            send_sem=send_sem.at[index],
+            recv_sem=recv_sem.at[index],
+            device_id=peer,
+            device_id_type=pl.DeviceIdType.MESH,
+        )
+        copy.start()
+        started.append(copy)
+        return copy
+
+    def gather_x(slot):
+        piece = tokens.at[slot, here, first]
+        return send(piece, piece, by_x)
+
+    def gather_y(dz):
+        return send(tokens.at[dz, here, first], tokens.at[4 + dz, here, first], by_y)
+
+    def gather_y_last(dz):
+        return send(tokens.at[dz, :, last], tokens.at[4 + dz, :, last], by_y)
+
+    def gather_core(slot):
+        return send(tokens.at[slot], tokens.at[8 + slot], by_core)
+
+    x_last = send(tokens.at[0, here, last], tokens.at[0, here, last], by_x)
+    z_first = [None] + [
+        send(tokens.at[0, here, first], tokens.at[dz, here, first], by_z[dz]) for dz in (1, 2, 3)
+    ]
+    y_first = [gather_y(0)]
+    x_first = [gather_x(0)]
+    x_last.wait_recv()
+    z_last = [None] + [
+        send(tokens.at[0, :, last], tokens.at[dz, :, last], by_z[dz]) for dz in (1, 2, 3)
+    ]
+    y_last = [gather_y_last(0)]
+    for dz in (1, 2, 3):
+        z_first[dz].wait_recv()
+        y_first.append(gather_y(dz))
+        x_first.append(gather_x(dz))
+    x_first[0].wait_recv()
+    to_core = [gather_core(0)]
+    for dz in (1, 2, 3):
+        z_last[dz].wait_recv()
+        y_last.append(gather_y_last(dz))
+    for dz in range(4):
+        y_first[dz].wait_recv()
+        x_first.append(gather_x(4 + dz))
+    for dz in (1, 2, 3):
+        x_first[dz].wait_recv()
+        to_core.append(gather_core(dz))
+
+    expert_row = lax.broadcasted_iota(jnp.int32, (experts, count), 0) == place
+    slot_row = lax.broadcasted_iota(jnp.int32, (capacity, count), 0)
+
+    def experts_on(base):
+        for step in range(BATCH):
+            slot = base + step
+            request = moved(slot % 4, (slot // 4) % 2, slot // 8)
+            slots = slots_ref[request]
+            halves = [tokens[slot, 0], tokens[slot, 1]]
+            logits = sum(
+                lax.dot_general(
+                    router_ref[:, half * width : (half + 1) * width],
+                    halves[half],
+                    (((1,), (1,)), ((), ())),
+                    preferred_element_type=jnp.float32,
+                )
+                for half in (0, 1)
+            )
+            logits = jnp.where(slots >= 0.0, logits, MASKED)
+            raised = jnp.exp(logits - jnp.max(logits, axis=0, keepdims=True))
+            share = raised / jnp.sum(raised, axis=0, keepdims=True)
+            weight = jnp.sum(jnp.where(expert_row, share, 0.0), axis=0, keepdims=True)
+            mine = jnp.sum(jnp.where(expert_row, slots, 0.0), axis=0, keepdims=True)
+            chosen = slot_row == mine.astype(jnp.int32)
+            combine[step] = jnp.where(chosen, weight, 0.0).astype(jnp.bfloat16)
+            select = jnp.where(chosen, 1.0, 0.0).astype(jnp.bfloat16)
+            for half in (0, 1):
+                rows_in[step * capacity : (step + 1) * capacity, half * width : (half + 1) * width] = (
+                    jnp.dot(select, halves[half], preferred_element_type=jnp.float32).astype(
+                        jnp.bfloat16
+                    )
+                )
+        units = hidden.shape[1]
+        for start in range(0, units, 256):
+            stop = min(start + 256, units)
+            gate_value = jnp.dot(
+                rows_in[...], gate_up[0, :, start:stop], preferred_element_type=jnp.float32
+            )
+            up_value = jnp.dot(
+                rows_in[...], gate_up[1, :, start:stop], preferred_element_type=jnp.float32
+            )
+            hidden[:, start:stop] = (gate_value / (1.0 + jnp.exp(-gate_value)) * up_value).astype(
+                jnp.bfloat16
+            )
+        for half in (0, 1):
+            for start in range(0, width, 512):
+                stop = min(start + 512, width)
+                answered = jnp.dot(
+                    hidden[...],
+                    down[:, half * width + start : half * width + stop],
+                    preferred_element_type=jnp.float32,
+                ).astype(jnp.bfloat16)
+                for step in range(BATCH):
+                    partial[base + step, half, :, start:stop] = lax.dot_general(
+                        combine[step],
+                        answered[step * capacity : (step + 1) * capacity],
+                        (((0,), (0,)), ((), ())),
+                        preferred_element_type=jnp.float32,
+                    ).astype(jnp.bfloat16)
+
+    def added(one, other):
+        return (one.astype(jnp.float32) + other.astype(jnp.float32)).astype(jnp.bfloat16)
+
+    def return_core(slot):
+        return send(partial.at[8 + slot], from_core.at[slot], by_core)
+
+    def return_x(slot):
+        return send(partial.at[slot, there, first], from_x.at[slot], by_x)
+
+    for one in weights:
+        one.wait()
+    experts_on(0)
+    for dz in range(4):
+        to_core[dz].wait_recv()
+    experts_on(8)
+    back_core = [return_core(dz) for dz in range(4)]
+    for dz in range(4):
+        x_first[4 + dz].wait_recv()
+        y_last[dz].wait_recv()
+        to_core.append(gather_core(4 + dz))
+    back_x = []
+    for dz in range(4):
+        back_core[dz].wait_recv()
+        partial[dz] = added(partial[dz], from_core[dz])
+        back_x.append(return_x(dz))
+    for dz in range(4):
+        to_core[4 + dz].wait_recv()
+    experts_on(12)
+    back_core += [return_core(4 + dz) for dz in range(4)]
+    experts_on(4)
+    back_y_last = []
+    for dz in range(4):
+        back_core[4 + dz].wait_recv()
+        partial[4 + dz] = added(partial[4 + dz], from_core[4 + dz])
+        back_y_last.append(send(partial.at[4 + dz, :, last], from_y_last.at[dz], by_y))
+        back_x.append(return_x(4 + dz))
+    back_y = []
+    for dz in range(4):
+        back_x[4 + dz].wait_recv()
+        partial[4 + dz, here, :FIRST] = added(partial[4 + dz, here, :FIRST], from_x[4 + dz])
+        back_y.append(send(partial.at[4 + dz, here, first], from_y.at[dz], by_y))
+    back_z_last = [None]
+    for dz in (1, 2, 3):
+        back_y_last[dz].wait_recv()
+        partial[dz, :, FIRST:] = added(partial[dz, :, FIRST:], from_y_last[dz])
+        back_z_last.append(send(partial.at[dz, :, last], from_z_last.at[dz - 1], by_z[dz]))
+    back_z = [None]
+    for dz in (1, 2, 3):
+        back_x[dz].wait_recv()
+        back_y[dz].wait_recv()
+        partial[dz, here, :FIRST] = (
+            partial[dz, here, :FIRST].astype(jnp.float32)
+            + from_x[dz].astype(jnp.float32)
+            + from_y[dz].astype(jnp.float32)
+        ).astype(jnp.bfloat16)
+        back_z.append(send(partial.at[dz, here, first], from_z.at[dz - 1], by_z[dz]))
+    back_y_last[0].wait_recv()
+    for dz in (1, 2, 3):
+        back_z_last[dz].wait_recv()
+
+    def last_sum(half):
+        total = partial[0, half, FIRST:].astype(jnp.float32) + from_y_last[0, half].astype(
+            jnp.float32
+        )
+        for dz in (1, 2, 3):
+            total = total + from_z_last[dz - 1, half].astype(jnp.float32)
+        return total
+
+    partial[0, there, FIRST:] = last_sum(there).astype(jnp.bfloat16)
+    back_x_last = send(partial.at[0, there, last], from_x_last, by_x)
+    back_x[0].wait_recv()
+    back_y[0].wait_recv()
+    for dz in (1, 2, 3):
+        back_z[dz].wait_recv()
+    total = (
+        partial[0, here, :FIRST].astype(jnp.float32)
+        + from_x[0].astype(jnp.float32)
+        + from_y[0].astype(jnp.float32)
+    )
+    for dz in (1, 2, 3):
+        total = total + from_z[dz - 1].astype(jnp.float32)
+    out_ref[:FIRST] = total.astype(jnp.bfloat16)
+    total = last_sum(here)
+    back_x_last.wait_recv()
+    out_ref[FIRST:] = (total + from_x_last[...].astype(jnp.float32)).astype(jnp.bfloat16)
+    for copy in started:
+        copy.wait_send()
+
+
+def exchange(normed_cols, slots, router_rows, w_gate_up, w_down, capacity):
+    count, width = normed_cols.shape
+    units = w_gate_up.shape[-1]
+    rest = count - FIRST
+    low = jnp.bfloat16
+    vmem = pl.BlockSpec(memory_space=pltpu.VMEM)
+    hbm = pl.BlockSpec(memory_space=pl.ANY)
+    return pl.pallas_call(
+        exchange_kernel,
+        out_shape=jax.ShapeDtypeStruct((count, width), low),
+        in_specs=[vmem, vmem, vmem, hbm, hbm],
+        out_specs=vmem,
+        scratch_shapes=[
+            pltpu.VMEM((16, 2, count, width), low),
+            pltpu.VMEM((16, 2, count, width), low),
+            pltpu.VMEM((8, 2, count, width), low),
+            pltpu.VMEM((8, FIRST, width), low),
+            pltpu.VMEM((rest, width), low),
+            pltpu.VMEM((4, FIRST, width), low),
+            pltpu.VMEM((4, 2, rest, width), low),
+            pltpu.VMEM((3, FIRST, width), low),
+            pltpu.VMEM((3, 2, rest, width), low),
+            pltpu.VMEM((2, 2 * width, units), low),
+            pltpu.VMEM((units, 2 * width), low),
+            pltpu.VMEM((BATCH * capacity, 2 * width), low),
+            pltpu.VMEM((BATCH * capacity, units), low),
+            pltpu.VMEM((BATCH, capacity, count), low),
+            pltpu.SemaphoreType.DMA((2,)),
+            pltpu.SemaphoreType.DMA((62,)),
+            pltpu.SemaphoreType.DMA((62,)),
+        ],
+        compiler_params=pltpu.CompilerParams(
+            collective_id=0, has_side_effects=True, vmem_limit_bytes=56 * 1024 * 1024
+        ),
+        cost_estimate=pl.CostEstimate(
+            flops=10_000_000_000, bytes_accessed=10_000_000, transcendentals=1_000_000
+        ),
+    )(normed_cols, slots, router_rows, w_gate_up, w_down)
+
+
+def slot_table(routes, experts_all):
+    tokens_here = routes.shape[0]
+    hits = jnp.any(
+        routes[None, :, :] == jnp.arange(experts_all, dtype=jnp.int32)[:, None, None], axis=2
+    )
+    position = jnp.arange(tokens_here, dtype=jnp.int32)
+    earlier = (position[:, None] < position[None, :]).astype(jnp.bfloat16)
+    slots = jnp.dot(hits.astype(jnp.bfloat16), earlier, preferred_element_type=jnp.float32)
+    return jnp.where(hits, slots, -1.0)
+
+
+def routed_body(
+    resid,
+    query,
+    key_new,
+    value_new,
+    cache_kv,
+    cache_len,
+    w_out,
+    norm_gain,
+    w_router,
+    routes,
+    w_gate_up,
+    w_down,
+):
+    tokens_here = query.shape[0]
+    heads_here = query.shape[1] // HD
+    experts_all = w_router.shape[1]
+    column_width = resid.shape[1]
+    table = lax.all_gather(slot_table(routes, experts_all), "ep", axis=0, tiled=False)
+    group_index = lax.axis_index("grp")
+    request = lax.axis_index("ep")
+    capacity = max(2, 8 * tokens_here // lax.axis_size("ep"))
+    score_scale = float(HD) ** (-0.5)
+    column_start = group_index * column_width
+    queries = query.reshape(tokens_here, heads_here, HD)
+    new_keys = key_new.reshape(tokens_here, heads_here, HD)
+    new_values = value_new.reshape(tokens_here, heads_here, HD)
+    cache_rows = cache_kv.shape[1]
+    cache_keys = cache_kv[0].reshape(cache_rows, heads_here, HD)
+    cache_values = cache_kv[1].reshape(cache_rows, heads_here, HD)
+    own_length = lax.dynamic_index_in_dim(cache_len, request, 0, keepdims=False)
+    position = jnp.arange(tokens_here, dtype=jnp.int32)
+    causal = (position[:, None] >= position[None, :])[:, None, :]
+    new_scores = (
+        jnp.einsum("qhd,khd->qhk", queries, new_keys, preferred_element_type=jnp.float32)
+        * score_scale
+    )
+    new_scores = jnp.where(causal, new_scores, MASKED)
+    live_rows = (jnp.arange(cache_rows, dtype=jnp.int32) < own_length)[None, None, :]
+    old_scores = (
+        jnp.einsum("qhd,khd->qhk", queries, cache_keys, preferred_element_type=jnp.float32)
+        * score_scale
+    )
+    old_scores = jnp.where(live_rows, old_scores, MASKED)
+    row_max = jnp.maximum(jnp.max(new_scores, axis=-1), jnp.max(old_scores, axis=-1))
+    new_probs = jnp.exp(new_scores - row_max[..., None])
+    old_probs = jnp.exp(old_scores - row_max[..., None])
+    denominator = jnp.sum(new_probs, axis=-1) + jnp.sum(old_probs, axis=-1)
+    weighted = jnp.einsum(
+        "qhk,khd->qhd",
+        new_probs.astype(jnp.bfloat16),
+        new_values,
+        preferred_element_type=jnp.float32,
+    )
+    weighted = weighted + jnp.einsum(
+        "qhk,khd->qhd",
+        old_probs.astype(jnp.bfloat16),
+        cache_values,
+        preferred_element_type=jnp.float32,
+    )
+    attended = (
+        (weighted / denominator[..., None])
+        .astype(jnp.bfloat16)
+        .reshape(tokens_here, heads_here * HD)
+    )
+    projected = jnp.dot(attended, w_out, preferred_element_type=jnp.float32)
+    attn_share = lax.psum_scatter(projected, "grp", scatter_dimension=1, tiled=True)
+    after_cols = (resid.astype(jnp.float32) + attn_share).astype(jnp.bfloat16)
+    after_wide = after_cols.astype(jnp.float32)
+    squares = lax.psum(jnp.sum(after_wide * after_wide, axis=1), "grp")
+    inverse = lax.rsqrt(squares / D + EPS)
+    gain_cols = lax.dynamic_slice_in_dim(norm_gain, column_start, column_width, 0)
+    normed_cols = (after_wide * inverse[:, None] * gain_cols.astype(jnp.float32)[None, :]).astype(
+        jnp.bfloat16
+    )
+    mixed_cols = exchange(normed_cols, table, w_router.T, w_gate_up, w_down, capacity)
+    return (after_cols, mixed_cols)
+
+
 def solution(mesh):
+    fits = mesh.shape["ep"] == 16 and mesh.shape["grp"] == 2
     return jax.shard_map(
-        body,
+        routed_body if fits else wide_body,
         mesh=mesh,
         in_specs=(
             P("ep", "grp"),

time: 317 us -> 186 us (0.59)
  waiting for transfers between devices: 127 us -> 0.02 us
  Pallas kernels: 0 us -> 109 us
  blocking collectives: 115 us -> 30 us
  matrix products: 29.4 us -> 7.53 us
  starting transfers between devices: 5.56 us -> 0.04 us
  other arithmetic: 6.94 us -> 3.76 us
    pallas_call x0 -> x1, Pallas kernels: none -> 109 us  [exchange(): pl.pallas_call(exchange_kernel, out_shape=jax.ShapeDtypeStruct((count, wi...]
    all_to_all x1 -> x0, blocking collectives: 97.8 us -> none  [body(): lax.all_to_all(outgoing, 'ep', split_axis=0, concat_axis=0, tiled=True)]
    all_to_all x1 -> x0, waiting for transfers between devices: 72.1 us -> none  [send_back(): lax.all_to_all(answered, 'ep', split_axis=0, concat_axis=0, tiled=True)]
    reduce_scatter x2 -> x1, waiting for transfers between devices: 55.2 us -> 0.01 us  [routed_body(): lax.psum_scatter(projected, 'grp', scatter_dimension=1, tiled=True)]
    dot_general x10 -> x6, matrix products: 29.4 us -> 7.53 us  [the longest x1 3.94 us: routed_body(): projected = jnp.dot(attended, w_out, preferred_element_type=jnp.float32)]
    all_gather x1, blocking collectives: 7.59 us -> 24.9 us  [routed_body(): lax.all_gather(slot_table(routes, experts_all), 'ep', axis=0, tiled=False)]
    unnamed x24 -> x21, local copies, waits for them, and re-layouts: 6.33 us -> 13.4 us
    all_to_all x1 -> x0, starting transfers between devices: 5.48 us -> none  [send_back(): lax.all_to_all(answered, 'ep', split_axis=0, concat_axis=0, tiled=True)]
  transfers between devices with their start and end apart: 3 -> 1, of which waited for: 3 -> 0; matrix products, arithmetic and copies ran while one was open for 1% -> 5% of each run, Pallas kernels for 0% -> 0%
where the time goes in v1:
time: 186 us; the launch traced here: 185 us
  Pallas kernels  109 us (59%)
  blocking collectives  30 us (16%)
  local copies, waits for them, and re-layouts  20.8 us (11%)
  between operations  14.2 us (8%)
  matrix products  7.53 us (4%)
  other arithmetic  3.76 us (2%)
    pallas_call x1, Pallas kernels, exchange(): pl.pallas_call(exchange_kernel, out_shape=jax.ShapeDtypeStruct((count, wi...  109 us
    all_gather x1, blocking collectives, routed_body(): lax.all_gather(slot_table(routes, experts_all), 'ep', axis=0, tiled=False)  24.9 us
    unnamed x21, local copies, waits for them, and re-layouts  13.4 us
    psum x1, blocking collectives, routed_body(): squares = lax.psum(jnp.sum(after_wide * after_wide, axis=1), 'grp')  5.13 us
    slice x1, local copies, waits for them, and re-layouts, routed_body(): cache_keys = cache_kv[0].reshape(cache_rows, heads_here, HD)  4.02 us
    dot_general x1, matrix products, routed_body(): projected = jnp.dot(attended, w_out, preferred_element_type=jnp.float32)  3.94 us
  transfers between devices with their start and end apart: 1, of which 0 were waited for; matrix products, arithmetic and copies ran while one was open for 5% of the time, Pallas kernels for 0%

profile of v1, /device:TPU:0, one launch (start us, length us, event | category | flops | bytes accessed | tf_op | source)
XLA Modules:
  0.0 185.4 jit_solution(3474010741278818346)
XLA Ops:
  7.2 0.0 reduce-scatter.2.cloned.1.call-start
  7.3 4.0 %fusion.31 = (bf16[1,1024,1024]{2,1,0:T(8,128)(2,1)}, bf16[1,1024,1024]{2,1,0:T(8,128)(2,1)S(1)}) fusion(bf16[2,1024,1024]{2,1,0:T(8,128)(2,1)} %param.16), kind=kLoop, calls=%fused_computation.45 | loop fusion | bytes 8388608 | tf_op jit(solution)/shard_map/slice | solution.py:495
  11.3 2.6 %copy.41 = bf16[1,1024,1024]{1,2,0:T(8,128)(2,1)} copy(bf16[1,1024,1024]{2,1,0:T(8,128)(2,1)S(1)} %get-tuple-element.5) | data formatting | bytes 4194304 | tf_op jit(solution)/shard_map/slice | solution.py:496
  13.9 0.6 dynamic_slice.7
  14.4 0.6 iota_compare_fusion.4
  15.1 2.9 %copy.48 = bf16[1,1024,1024]{1,2,0:T(8,128)(2,1)S(1)} copy(bf16[1,1024,1024]{2,1,0:T(8,128)(2,1)} %get-tuple-element.4) | data formatting | bytes 4194304
  18.0 1.3 bitcast_reduce_fusion
  19.3 0.3 fusion.32
  19.7 0.9 fusion.1
  20.6 0.3 copy-done.1
  20.9 1.6 fusion.3
  22.5 0.2 copy.47
  22.7 0.1 fusion.17
  22.8 0.2 fusion.13
  23.0 3.9 %fusion.33 = f32[128,2048]{1,0:T(8,128)} fusion(bf16[128,1024]{0,1:T(8,128)(2,1)S(1)} %bitcast.61, bf16[1024,2048]{1,0:T(8,128)(2,1)} %param.18), kind=kOutput, calls=%fused_computation.47 | convolution fusion | flops 536870912 | bytes 5505024 | tf_op jit(solution)/shard_map/dot_general | solution.py:532
  27.0 0.0 reduce-scatter.2.cloned.1.call-update
  27.0 8.6 %copy.43.gate_up_hbm = bf16[1,2,2048,704]{3,2,1,0:T(8,128)(2,1)} copy(bf16[1,2,2048,704]{2,3,1,0:T(8,128)(2,1)} %param.22) | data formatting | bytes 11534336 | tf_op args[10]
  35.6 0.1 convolution_select_fusion
  35.8 24.9 %all-gather = f32[256,128]{1,0:T(8,128)} all-gather(f32[16,128]{1,0:T(8,128)S(1)} %convolution_select_fusion), channel_id=2, replica_groups=mesh['grp'=2,'ep'=16] {'ep'}, dimensions={0}, use_global_device_ids=true | all-gather | bytes 139264 | tf_op jit(solution)/shard_map/all_gather | solution.py:485
  60.6 1.2 fusion.14
  61.8 5.1 %psum.7 = f32[128]{0:T(128)S(1)} all-reduce(f32[128]{0:T(128)S(1)} %get-tuple-element.2), channel_id=1, replica_groups=mesh['grp'=2,'ep'=16] {'grp'}, use_global_device_ids=true, to_apply=%region_6.7 | all-reduce | flops 128 | bytes 1024 | tf_op jit(solution)/shard_map/psum | solution.py:536
  67.0 0.8 fusion.16.normed_ref
  67.8 109.1 %shard_map.131 = bf16[128,1024]{1,0:T(8,128)(2,1)} custom-call(bf16[128,1024]{1,0:T(8,128)(2,1)} %fusion.16.normed_ref, f32[16,16,128]{2,1,0:T(8,128)} %bitcast.62, bf16[16,2048]{1,0:T(8,128)(2,1)} %bitcast.63, bf16[1,2,2048,704]{3,2,1,0:T(8,128)(2,1)} %copy.43.gate_up_hbm, bf16[1,704,2048]{2,1,0:T(8,128)(2,1)} %down_hbm.1), custom_call_target="tpu_custom_call" | custom-call | flops 10000000000 | bytes 10000000 | tf_op jit(solution)/shard_map/pallas_call | solution.py:423
  176.9 1.7 copy.70
  (24 shorter events, 0.1 us)
Async XLA Ops:
  7.2 10.8 %copy-start = (bf16[128,1024]{1,0:T(8,128)(2,1)S(1)}, bf16[128,1024]{1,0:T(8,128)(2,1)}, u32[]{:S(2)}) copy-start(bf16[128,1024]{1,0:T(8,128)(2,1)} %param.13) | copy-start | bytes 786436
  7.2 53.5 %reduce-scatter.2.cloned.1.call-start = ((), (), s32[]{:S(2)}) async-start(), calls=%async_computation.1 | async-start | bytes 1572864 | tf_op jit(solution)/shard_map/reduce_scatter | solution.py:533
  11.3 2.6 %copy-start.8 = (s32[16]{0:T(128)S(1)}, s32[16]{0:T(128)}, u32[]{:S(2)}) copy-start(s32[16]{0:T(128)} %param.17) | copy-start | bytes 196
  18.0 1.3 copy-start.7
  19.3 1.6 copy-start.1
  20.6 1.9 %copy-start.3 = (bf16[128,1024]{1,0:T(8,128)(2,1)S(1)}, bf16[128,1024]{1,0:T(8,128)(2,1)}, u32[]{:S(2)}) copy-start(bf16[128,1024]{1,0:T(8,128)(2,1)} %param.15) | copy-start | bytes 786436
  27.0 8.6 %copy-start.5 = (s32[128,4]{0,1:T(4,128)S(1)}, s32[128,4]{0,1:T(4,128)}, u32[]{:S(2)}) copy-start(s32[128,4]{0,1:T(4,128)} %param.21) | copy-start | bytes 6148
  27.0 33.6 %copy-start.6 = (bf16[2048]{0:T(1024)(128)(2,1)S(1)}, bf16[2048]{0:T(1024)(128)(2,1)}, u32[]{:S(2)}) copy-start(bf16[2048]{0:T(1024)(128)(2,1)} %param.19) | copy-start | bytes 12292
  27.0 33.6 %copy-start.4 = (bf16[128,1024]{1,0:T(8,128)(2,1)S(1)}, bf16[128,1024]{1,0:T(8,128)(2,1)}, u32[]{:S(2)}) copy-start(bf16[128,1024]{1,0:T(8,128)(2,1)} %param.12) | copy-start | bytes 786436
  61.8 115.1 %copy-start.2 = (bf16[128,1024]{1,0:T(8,128)(2,1)}, bf16[128,1024]{1,0:T(8,128)(2,1)S(1)}, u32[]{:S(2)}) copy-start(bf16[128,1024]{1,0:T(8,128)(2,1)S(1)} %get-tuple-element.12) | copy-start | bytes 786436
Sparse Core Ops, SparseCore 0:
  27.1 22.9 reduce-scatter.1

commit v2 on v1

--- a/solution.py
+++ b/solution.py
@@ -142,13 +142,29 @@
 BATCH = 4
 
 
-def exchange_kernel(
-    normed_ref,
+def layer_kernel(
+    length_ref,
+    resid_ref,
+    query_ref,
+    key_ref,
+    value_ref,
+    gain_ref,
     slots_ref,
     router_ref,
+    cache_hbm,
+    project_hbm,
     gate_up_hbm,
     down_hbm,
+    after_ref,
     out_ref,
+    cache,
+    project,
+    attended,
+    share_out,
+    share_in,
+    squares_out,
+    squares_in,
+    slots_all,
     tokens,
     partial,
     from_core,
@@ -167,8 +183,7 @@
     send_sem,
     recv_sem,
 ):
-    count = normed_ref.shape[0]
-    width = normed_ref.shape[1]
+    count, width = resid_ref.shape
     capacity = combine.shape[1]
     experts = router_ref.shape[0]
     here = lax.axis_index("grp")
@@ -191,11 +206,21 @@
     by_core = (here, moved(0, 0, 1))
     by_z = [None] + [(here, moved(dz, 0, 0)) for dz in (1, 2, 3)]
 
+    keys = pltpu.make_async_copy(cache_hbm.at[0], cache.at[0], weight_sem.at[0])
+    values = pltpu.make_async_copy(cache_hbm.at[1], cache.at[1], weight_sem.at[1])
+    projection = [
+        pltpu.make_async_copy(
+            project_hbm.at[:, half * width : (half + 1) * width],
+            project.at[half],
+            weight_sem.at[2 + half],
+        )
+        for half in (0, 1)
+    ]
     weights = [
-        pltpu.make_async_copy(gate_up_hbm.at[0], gate_up, weight_sem.at[0]),
-        pltpu.make_async_copy(down_hbm.at[0], down, weight_sem.at[1]),
+        pltpu.make_async_copy(gate_up_hbm.at[0], gate_up, weight_sem.at[4]),
+        pltpu.make_async_copy(down_hbm.at[0], down, weight_sem.at[5]),
     ]
-    for one in weights:
+    for one in [keys, values] + projection + weights:
         one.start()
 
     barrier = pltpu.get_barrier_semaphore()
@@ -203,7 +228,7 @@
     for peer in peers:
         pl.semaphore_signal(barrier, inc=1, device_id=peer, device_id_type=pl.DeviceIdType.MESH)
 
-    tokens[0, here] = normed_ref[...]
+    slots_all[0] = slots_ref[...]
     pl.semaphore_wait(barrier, len(peers))
 
     first = pl.ds(0, FIRST)
@@ -237,47 +262,125 @@
     def gather_core(slot):
         return send(tokens.at[slot], tokens.at[8 + slot], by_core)
 
+    slots_z = [
+        send(slots_all.at[0], slots_all.at[dz], by_z[dz]) for dz in (1, 2, 3)
+    ]
+    slots_y = [send(slots_all.at[0], slots_all.at[4], by_y)]
+
+    score_scale = float(HD) ** (-0.5)
+    live_rows = (
+        lax.broadcasted_iota(jnp.int32, (count, cache.shape[1]), 1) < length_ref[place]
+    )
+    causal = lax.broadcasted_iota(jnp.int32, (count, count), 0) >= lax.broadcasted_iota(
+        jnp.int32, (count, count), 1
+    )
+    along_last = (((1,), (1,)), ((), ()))
+    keys.wait()
+    values.wait()
+    for start in range(0, width, HD):
+        columns = slice(start, start + HD)
+        asked = query_ref[:, columns]
+        new_scores = score_scale * lax.dot_general(
+            asked, key_ref[:, columns], along_last, preferred_element_type=jnp.float32
+        )
+        old_scores = score_scale * lax.dot_general(
+            asked, cache[0, :, columns], along_last, preferred_element_type=jnp.float32
+        )
+        new_scores = jnp.where(causal, new_scores, MASKED)
+        old_scores = jnp.where(live_rows, old_scores, MASKED)
+        row_max = jnp.maximum(
+            jnp.max(new_scores, axis=1, keepdims=True), jnp.max(old_scores, axis=1, keepdims=True)
+        )
+        new_probs = jnp.exp(new_scores - row_max)
+        old_probs = jnp.exp(old_scores - row_max)
+        denominator = jnp.sum(new_probs, axis=1, keepdims=True) + jnp.sum(
+            old_probs, axis=1, keepdims=True
+        )
+        weighted = jnp.dot(
+            new_probs.astype(jnp.bfloat16),
+            value_ref[:, columns],
+            preferred_element_type=jnp.float32,
+        ) + jnp.dot(
+            old_probs.astype(jnp.bfloat16),
+            cache[1, :, columns],
+            preferred_element_type=jnp.float32,
+        )
+        attended[:, columns] = (weighted / denominator).astype(jnp.bfloat16)
+
+    for one in projection:
+        one.wait()
+    share_out[...] = jnp.dot(
+        attended[...], project[there], preferred_element_type=jnp.float32
+    ).astype(jnp.bfloat16)
+    share = send(share_out, share_in, by_x)
+    for dz in (1, 2, 3):
+        slots_z[dz - 1].wait_recv()
+        slots_y.append(send(slots_all.at[dz], slots_all.at[4 + dz], by_y))
+    own_share = jnp.dot(attended[...], project[here], preferred_element_type=jnp.float32)
+    slots_core = [send(slots_all.at[dz], slots_all.at[8 + dz], by_core) for dz in range(4)]
+    for dz in range(4):
+        slots_y[dz].wait_recv()
+        slots_core.append(send(slots_all.at[4 + dz], slots_all.at[12 + dz], by_core))
+    share.wait_recv()
+    after = (
+        resid_ref[...].astype(jnp.float32) + (own_share + share_in[...].astype(jnp.float32))
+    ).astype(jnp.bfloat16)
+    after_ref[...] = after
+    after = after.astype(jnp.float32)
+    squares = jnp.sum(after * after, axis=1, keepdims=True)
+    squares_out[...] = jnp.transpose(jnp.broadcast_to(squares, (count, 128)))[:8]
+    squares_sent = send(squares_out, squares_in, by_x)
+    squares_sent.wait_recv()
+    squares = squares + jnp.transpose(jnp.broadcast_to(squares_in[:1], (128, count)))[:, :1]
+    inverse = lax.rsqrt(squares / (2 * width) + EPS)
+    tokens[0, here] = (after * inverse * gain_ref[here].astype(jnp.float32)).astype(jnp.bfloat16)
+
     x_last = send(tokens.at[0, here, last], tokens.at[0, here, last], by_x)
-    z_first = [None] + [
-        send(tokens.at[0, here, first], tokens.at[dz, here, first], by_z[dz]) for dz in (1, 2, 3)
-    ]
     y_first = [gather_y(0)]
-    x_first = [gather_x(0)]
+    x_first = {0: gather_x(0)}
+    z_first = [None]
+    z_last = [None]
+    y_last = []
+    to_core = {}
+    z_first.append(send(tokens.at[0, here, first], tokens.at[1, here, first], by_z[1]))
     x_last.wait_recv()
-    z_last = [None] + [
-        send(tokens.at[0, :, last], tokens.at[dz, :, last], by_z[dz]) for dz in (1, 2, 3)
-    ]
-    y_last = [gather_y_last(0)]
     for dz in (1, 2, 3):
+        if dz > 1:
+            z_first.append(send(tokens.at[0, here, first], tokens.at[dz, here, first], by_z[dz]))
+        z_last.append(send(tokens.at[0, :, last], tokens.at[dz, :, last], by_z[dz]))
+    y_last.append(gather_y_last(0))
+
+    def arrive_z(dz):
         z_first[dz].wait_recv()
         y_first.append(gather_y(dz))
-        x_first.append(gather_x(dz))
-    x_first[0].wait_recv()
-    to_core = [gather_core(0)]
-    for dz in (1, 2, 3):
+        x_first[dz] = gather_x(dz)
         z_last[dz].wait_recv()
         y_last.append(gather_y_last(dz))
-    for dz in range(4):
+
+    def arrive_y(dz):
         y_first[dz].wait_recv()
-        x_first.append(gather_x(4 + dz))
-    for dz in (1, 2, 3):
+        x_first[4 + dz] = gather_x(4 + dz)
         x_first[dz].wait_recv()
-        to_core.append(gather_core(dz))
+        to_core[dz] = gather_core(dz)
+
+    def arrive_x(dz):
+        x_first[4 + dz].wait_recv()
+        y_last[dz].wait_recv()
+        to_core[4 + dz] = gather_core(4 + dz)
 
     expert_row = lax.broadcasted_iota(jnp.int32, (experts, count), 0) == place
     slot_row = lax.broadcasted_iota(jnp.int32, (capacity, count), 0)
 
-    def experts_on(base):
+    def experts_on(dz):
         for step in range(BATCH):
-            slot = base + step
-            request = moved(slot % 4, (slot // 4) % 2, slot // 8)
-            slots = slots_ref[request]
+            slot = dz + 4 * step
+            slots = slots_all[slot]
             halves = [tokens[slot, 0], tokens[slot, 1]]
             logits = sum(
                 lax.dot_general(
                     router_ref[:, half * width : (half + 1) * width],
                     halves[half],
-                    (((1,), (1,)), ((), ())),
+                    along_last,
                     preferred_element_type=jnp.float32,
                 )
                 for half in (0, 1)
@@ -299,11 +402,17 @@
         units = hidden.shape[1]
         for start in range(0, units, 256):
             stop = min(start + 256, units)
-            gate_value = jnp.dot(
-                rows_in[...], gate_up[0, :, start:stop], preferred_element_type=jnp.float32
+            gate_value = lax.dot_general(
+                rows_in[...],
+                gate_up[0, start:stop],
+                along_last,
+                preferred_element_type=jnp.float32,
             )
-            up_value = jnp.dot(
-                rows_in[...], gate_up[1, :, start:stop], preferred_element_type=jnp.float32
+            up_value = lax.dot_general(
+                rows_in[...],
+                gate_up[1, start:stop],
+                along_last,
+                preferred_element_type=jnp.float32,
             )
             hidden[:, start:stop] = (gate_value / (1.0 + jnp.exp(-gate_value)) * up_value).astype(
                 jnp.bfloat16
@@ -317,7 +426,7 @@
                     preferred_element_type=jnp.float32,
                 ).astype(jnp.bfloat16)
                 for step in range(BATCH):
-                    partial[base + step, half, :, start:stop] = lax.dot_general(
+                    partial[dz + 4 * step, half, :, start:stop] = lax.dot_general(
                         combine[step],
                         answered[step * capacity : (step + 1) * capacity],
                         (((0,), (0,)), ((), ())),
@@ -333,45 +442,37 @@
     def return_x(slot):
         return send(partial.at[slot, there, first], from_x.at[slot], by_x)
 
-    for one in weights:
-        one.wait()
-    experts_on(0)
-    for dz in range(4):
+    back_core = {}
+    back_x = {}
+    back_y = {}
+    back_y_last = {}
+    back_z = {}
+    back_z_last = {}
+
+    def answer(dz):
         to_core[dz].wait_recv()
-    experts_on(8)
-    back_core = [return_core(dz) for dz in range(4)]
-    for dz in range(4):
-        x_first[4 + dz].wait_recv()
-        y_last[dz].wait_recv()
-        to_core.append(gather_core(4 + dz))
-    back_x = []
-    for dz in range(4):
-        back_core[dz].wait_recv()
-        partial[dz] = added(partial[dz], from_core[dz])
-        back_x.append(return_x(dz))
-    for dz in range(4):
         to_core[4 + dz].wait_recv()
-    experts_on(12)
-    back_core += [return_core(4 + dz) for dz in range(4)]
-    experts_on(4)
-    back_y_last = []
-    for dz in range(4):
-        back_core[4 + dz].wait_recv()
-        partial[4 + dz] = added(partial[4 + dz], from_core[4 + dz])
-        back_y_last.append(send(partial.at[4 + dz, :, last], from_y_last.at[dz], by_y))
-        back_x.append(return_x(4 + dz))
-    back_y = []
-    for dz in range(4):
+        experts_on(dz)
+        for slot in (4 + dz, dz):
+            back_core[slot] = return_core(slot)
+
+    def core_sum(dz):
+        for slot in (4 + dz, dz):
+            back_core[slot].wait_recv()
+            partial[slot] = added(partial[slot], from_core[slot])
+            back_x[slot] = return_x(slot)
+            if slot >= 4:
+                back_y_last[dz] = send(partial.at[slot, :, last], from_y_last.at[dz], by_y)
+
+    def x_sum(dz):
         back_x[4 + dz].wait_recv()
         partial[4 + dz, here, :FIRST] = added(partial[4 + dz, here, :FIRST], from_x[4 + dz])
-        back_y.append(send(partial.at[4 + dz, here, first], from_y.at[dz], by_y))
-    back_z_last = [None]
-    for dz in (1, 2, 3):
+        back_y[dz] = send(partial.at[4 + dz, here, first], from_y.at[dz], by_y)
+
+    def y_sum(dz):
         back_y_last[dz].wait_recv()
         partial[dz, :, FIRST:] = added(partial[dz, :, FIRST:], from_y_last[dz])
-        back_z_last.append(send(partial.at[dz, :, last], from_z_last.at[dz - 1], by_z[dz]))
-    back_z = [None]
-    for dz in (1, 2, 3):
+        back_z_last[dz] = send(partial.at[dz, :, last], from_z_last.at[dz - 1], by_z[dz])
         back_x[dz].wait_recv()
         back_y[dz].wait_recv()
         partial[dz, here, :FIRST] = (
@@ -379,7 +480,38 @@
             + from_x[dz].astype(jnp.float32)
             + from_y[dz].astype(jnp.float32)
         ).astype(jnp.bfloat16)
-        back_z.append(send(partial.at[dz, here, first], from_z.at[dz - 1], by_z[dz]))
+        back_z[dz] = send(partial.at[dz, here, first], from_z.at[dz - 1], by_z[dz])
+
+    arrive_y(0)
+    arrive_z(1)
+    arrive_x(0)
+    arrive_y(1)
+    for one in slots_core:
+        one.wait_recv()
+    for one in weights:
+        one.wait()
+    answer(0)
+    arrive_z(2)
+    arrive_x(1)
+    arrive_y(2)
+    core_sum(0)
+    answer(1)
+    arrive_z(3)
+    arrive_x(2)
+    arrive_y(3)
+    core_sum(1)
+    x_sum(0)
+    answer(2)
+    arrive_x(3)
+    x_sum(1)
+    core_sum(2)
+    y_sum(1)
+    answer(3)
+    x_sum(2)
+    core_sum(3)
+    y_sum(2)
+    x_sum(3)
+    y_sum(3)
     back_y_last[0].wait_recv()
     for dz in (1, 2, 3):
         back_z_last[dz].wait_recv()
@@ -413,19 +545,43 @@
         copy.wait_send()
 
 
-def exchange(normed_cols, slots, router_rows, w_gate_up, w_down, capacity):
-    count, width = normed_cols.shape
-    units = w_gate_up.shape[-1]
+def layer(
+    lengths,
+    resid,
+    query,
+    key_new,
+    value_new,
+    gain,
+    slots,
+    router_rows,
+    cache_kv,
+    w_out,
+    gate_up_rows,
+    w_down,
+    capacity,
+):
+    count, width = resid.shape
+    units = w_down.shape[1]
     rest = count - FIRST
     low = jnp.bfloat16
+    wide = jnp.float32
     vmem = pl.BlockSpec(memory_space=pltpu.VMEM)
     hbm = pl.BlockSpec(memory_space=pl.ANY)
+    block = jax.ShapeDtypeStruct((count, width), low)
     return pl.pallas_call(
-        exchange_kernel,
-        out_shape=jax.ShapeDtypeStruct((count, width), low),
-        in_specs=[vmem, vmem, vmem, hbm, hbm],
-        out_specs=vmem,
+        layer_kernel,
+        out_shape=(block, block),
+        in_specs=[pl.BlockSpec(memory_space=pltpu.SMEM)] + [vmem] * 7 + [hbm] * 4,
+        out_specs=(vmem, vmem),
         scratch_shapes=[
+            pltpu.VMEM(cache_kv.shape, low),
+            pltpu.VMEM((2, width, width), low),
+            pltpu.VMEM((count, width), low),
+            pltpu.VMEM((count, width), low),
+            pltpu.VMEM((count, width), low),
+            pltpu.VMEM((8, count), wide),
+            pltpu.VMEM((8, count), wide),
+            pltpu.VMEM((16,) + slots.shape, wide),
             pltpu.VMEM((16, 2, count, width), low),
             pltpu.VMEM((16, 2, count, width), low),
             pltpu.VMEM((8, 2, count, width), low),
@@ -435,28 +591,41 @@
             pltpu.VMEM((4, 2, rest, width), low),
             pltpu.VMEM((3, FIRST, width), low),
             pltpu.VMEM((3, 2, rest, width), low),
-            pltpu.VMEM((2, 2 * width, units), low),
+            pltpu.VMEM((2, units, 2 * width), low),
             pltpu.VMEM((units, 2 * width), low),
             pltpu.VMEM((BATCH * capacity, 2 * width), low),
             pltpu.VMEM((BATCH * capacity, units), low),
             pltpu.VMEM((BATCH, capacity, count), low),
-            pltpu.SemaphoreType.DMA((2,)),
-            pltpu.SemaphoreType.DMA((62,)),
-            pltpu.SemaphoreType.DMA((62,)),
+            pltpu.SemaphoreType.DMA((6,)),
+            pltpu.SemaphoreType.DMA((79,)),
+            pltpu.SemaphoreType.DMA((79,)),
         ],
         compiler_params=pltpu.CompilerParams(
-            collective_id=0, has_side_effects=True, vmem_limit_bytes=56 * 1024 * 1024
+            collective_id=0, has_side_effects=True, vmem_limit_bytes=60 * 1024 * 1024
         ),
         cost_estimate=pl.CostEstimate(
-            flops=10_000_000_000, bytes_accessed=10_000_000, transcendentals=1_000_000
+            flops=12_000_000_000, bytes_accessed=18_000_000, transcendentals=2_000_000
         ),
-    )(normed_cols, slots, router_rows, w_gate_up, w_down)
+    )(
+        lengths,
+        resid,
+        query,
+        key_new,
+        value_new,
+        gain,
+        slots,
+        router_rows,
+        cache_kv,
+        w_out,
+        gate_up_rows,
+        w_down,
+    )
 
 
 def slot_table(routes, experts_all):
     tokens_here = routes.shape[0]
     hits = jnp.any(
-        routes[None, :, :] == jnp.arange(experts_all, dtype=jnp.int32)[:, None, None], axis=2
+        routes.T[None, :, :] == jnp.arange(experts_all, dtype=jnp.int32)[:, None, None], axis=1
     )
     position = jnp.arange(tokens_here, dtype=jnp.int32)
     earlier = (position[:, None] < position[None, :]).astype(jnp.bfloat16)
@@ -478,69 +647,24 @@
     w_gate_up,
     w_down,
 ):
-    tokens_here = query.shape[0]
-    heads_here = query.shape[1] // HD
     experts_all = w_router.shape[1]
-    column_width = resid.shape[1]
-    table = lax.all_gather(slot_table(routes, experts_all), "ep", axis=0, tiled=False)
-    group_index = lax.axis_index("grp")
-    request = lax.axis_index("ep")
-    capacity = max(2, 8 * tokens_here // lax.axis_size("ep"))
-    score_scale = float(HD) ** (-0.5)
-    column_start = group_index * column_width
-    queries = query.reshape(tokens_here, heads_here, HD)
-    new_keys = key_new.reshape(tokens_here, heads_here, HD)
-    new_values = value_new.reshape(tokens_here, heads_here, HD)
-    cache_rows = cache_kv.shape[1]
-    cache_keys = cache_kv[0].reshape(cache_rows, heads_here, HD)
-    cache_values = cache_kv[1].reshape(cache_rows, heads_here, HD)
-    own_length = lax.dynamic_index_in_dim(cache_len, request, 0, keepdims=False)
-    position = jnp.arange(tokens_here, dtype=jnp.int32)
-    causal = (position[:, None] >= position[None, :])[:, None, :]
-    new_scores = (
-        jnp.einsum("qhd,khd->qhk", queries, new_keys, preferred_element_type=jnp.float32)
-        * score_scale
-    )
-    new_scores = jnp.where(causal, new_scores, MASKED)
-    live_rows = (jnp.arange(cache_rows, dtype=jnp.int32) < own_length)[None, None, :]
-    old_scores = (
-        jnp.einsum("qhd,khd->qhk", queries, cache_keys, preferred_element_type=jnp.float32)
-        * score_scale
-    )
-    old_scores = jnp.where(live_rows, old_scores, MASKED)
-    row_max = jnp.maximum(jnp.max(new_scores, axis=-1), jnp.max(old_scores, axis=-1))
-    new_probs = jnp.exp(new_scores - row_max[..., None])
-    old_probs = jnp.exp(old_scores - row_max[..., None])
-    denominator = jnp.sum(new_probs, axis=-1) + jnp.sum(old_probs, axis=-1)
-    weighted = jnp.einsum(
-        "qhk,khd->qhd",
-        new_probs.astype(jnp.bfloat16),
-        new_values,
-        preferred_element_type=jnp.float32,
-    )
-    weighted = weighted + jnp.einsum(
-        "qhk,khd->qhd",
-        old_probs.astype(jnp.bfloat16),
-        cache_values,
-        preferred_element_type=jnp.float32,
-    )
-    attended = (
-        (weighted / denominator[..., None])
-        .astype(jnp.bfloat16)
-        .reshape(tokens_here, heads_here * HD)
-    )
-    projected = jnp.dot(attended, w_out, preferred_element_type=jnp.float32)
-    attn_share = lax.psum_scatter(projected, "grp", scatter_dimension=1, tiled=True)
-    after_cols = (resid.astype(jnp.float32) + attn_share).astype(jnp.bfloat16)
-    after_wide = after_cols.astype(jnp.float32)
-    squares = lax.psum(jnp.sum(after_wide * after_wide, axis=1), "grp")
-    inverse = lax.rsqrt(squares / D + EPS)
-    gain_cols = lax.dynamic_slice_in_dim(norm_gain, column_start, column_width, 0)
-    normed_cols = (after_wide * inverse[:, None] * gain_cols.astype(jnp.float32)[None, :]).astype(
-        jnp.bfloat16
-    )
-    mixed_cols = exchange(normed_cols, table, w_router.T, w_gate_up, w_down, capacity)
-    return (after_cols, mixed_cols)
+    width = resid.shape[1]
+    capacity = max(2, 8 * resid.shape[0] // lax.axis_size("ep"))
+    return layer(
+        cache_len,
+        resid,
+        query,
+        key_new,
+        value_new,
+        norm_gain.reshape(2, 1, width),
+        slot_table(routes, experts_all),
+        w_router.T,
+        cache_kv,
+        w_out,
+        jnp.swapaxes(w_gate_up, 2, 3),
+        w_down,
+        capacity,
+    )
 
 
 def solution(mesh):

time: 186 us -> 121 us (0.65)
  the two profiles are of different devices: /device:TPU:0 before, /device:TPU:8 now
where the time goes in v2:
time: 121 us
  Pallas kernels  115 us (95%)
  local copies, waits for them, and re-layouts  4.63 us (4%)
    pallas_call x1, Pallas kernels, layer(): pl.pallas_call(layer_kernel, out_shape=(block, block), in_specs=[pl.Block...  115 us
    unnamed x2, local copies, waits for them, and re-layouts  3.34 us

profile of v2, /device:TPU:8, one launch (start us, length us, event | category | flops | bytes accessed | tf_op | source)
XLA Modules:
  0.0 121.2 jit_solution(11892924409884039373)
XLA Ops:
  0.6 0.7 fusion
  1.3 0.7 convolution_select_fusion.slots_ref
  2.1 1.3 %reshape.9.gain_ref = bf16[2,1,1024]{2,1,0:T(2,128)(2,1)} reshape(bf16[2048]{0:T(1024)(128)(2,1)} %param.19) | data formatting | bytes 8192 | tf_op jit(solution)/shard_map/reshape | solution.py:659
  3.4 114.5 %shard_map.131 = (bf16[128,1024]{1,0:T(8,128)(2,1)}, bf16[128,1024]{1,0:T(8,128)(2,1)}) custom-call(s32[16]{0:T(128)} %length_ref.1, bf16[128,1024]{1,0:T(8,128)(2,1)} %resid_ref.1, bf16[128,1024]{1,0:T(8,128)(2,1)} %query_ref.1, bf16[128,1024]{1,0:T(8,128)(2,1)} %key_ref.1, bf16[128,1024]{1,0:T(8,128)(2,1)} %value_ref.1, ...), custom_call_target="tpu_custom_call" | custom-call | flops 12000000000 | bytes 18000000 | tf_op jit(solution)/shard_map/pallas_call | solution.py:571
  117.9 1.7 %copy.18 = bf16[128,1024]{1,0:T(8,128)(2,1)} copy(bf16[128,1024]{1,0:T(8,128)(2,1)} %get-tuple-element.4) | data formatting | bytes 524288
  119.6 1.7 %copy.19 = bf16[128,1024]{1,0:T(8,128)(2,1)} copy(bf16[128,1024]{1,0:T(8,128)(2,1)} %get-tuple-element.5) | data formatting | bytes 524288

commit v3 on v2

--- a/solution.py
+++ b/solution.py
@@ -164,7 +164,9 @@
     share_in,
     squares_out,
     squares_in,
-    slots_all,
+    logits_out,
+    logits_in,
+    tables,
     tokens,
     partial,
     from_core,
@@ -228,7 +230,7 @@
     for peer in peers:
         pl.semaphore_signal(barrier, inc=1, device_id=peer, device_id_type=pl.DeviceIdType.MESH)
 
-    slots_all[0] = slots_ref[...]
+    tables[0, 0] = slots_ref[...]
     pl.semaphore_wait(barrier, len(peers))
 
     first = pl.ds(0, FIRST)
@@ -262,11 +264,6 @@
     def gather_core(slot):
         return send(tokens.at[slot], tokens.at[8 + slot], by_core)
 
-    slots_z = [
-        send(slots_all.at[0], slots_all.at[dz], by_z[dz]) for dz in (1, 2, 3)
-    ]
-    slots_y = [send(slots_all.at[0], slots_all.at[4], by_y)]
-
     score_scale = float(HD) ** (-0.5)
     live_rows = (
         lax.broadcasted_iota(jnp.int32, (count, cache.shape[1]), 1) < length_ref[place]
@@ -313,14 +310,7 @@
         attended[...], project[there], preferred_element_type=jnp.float32
     ).astype(jnp.bfloat16)
     share = send(share_out, share_in, by_x)
-    for dz in (1, 2, 3):
-        slots_z[dz - 1].wait_recv()
-        slots_y.append(send(slots_all.at[dz], slots_all.at[4 + dz], by_y))
     own_share = jnp.dot(attended[...], project[here], preferred_element_type=jnp.float32)
-    slots_core = [send(slots_all.at[dz], slots_all.at[8 + dz], by_core) for dz in range(4)]
-    for dz in range(4):
-        slots_y[dz].wait_recv()
-        slots_core.append(send(slots_all.at[4 + dz], slots_all.at[12 + dz], by_core))
     share.wait_recv()
     after = (
         resid_ref[...].astype(jnp.float32) + (own_share + share_in[...].astype(jnp.float32))
@@ -333,7 +323,9 @@
     squares_sent.wait_recv()
     squares = squares + jnp.transpose(jnp.broadcast_to(squares_in[:1], (128, count)))[:, :1]
     inverse = lax.rsqrt(squares / (2 * width) + EPS)
-    tokens[0, here] = (after * inverse * gain_ref[here].astype(jnp.float32)).astype(jnp.bfloat16)
+    half_here = pl.ds(pl.multiple_of(here * width, 128), width)
+    normed = (after * inverse * gain_ref[:, half_here]).astype(jnp.bfloat16)
+    tokens[0, here] = normed
 
     x_last = send(tokens.at[0, here, last], tokens.at[0, here, last], by_x)
     y_first = [gather_y(0)]
@@ -343,14 +335,29 @@
     y_last = []
     to_core = {}
     z_first.append(send(tokens.at[0, here, first], tokens.at[1, here, first], by_z[1]))
+    own_logits = lax.dot_general(
+        router_ref[:, half_here], normed, along_last, preferred_element_type=jnp.float32
+    )
+    logits_out[...] = own_logits
+    logits_sent = send(logits_out, logits_in, by_x)
     x_last.wait_recv()
     for dz in (1, 2, 3):
         if dz > 1:
             z_first.append(send(tokens.at[0, here, first], tokens.at[dz, here, first], by_z[dz]))
         z_last.append(send(tokens.at[0, :, last], tokens.at[dz, :, last], by_z[dz]))
     y_last.append(gather_y_last(0))
+    logits_sent.wait_recv()
+    logits = jnp.where(slots_ref[...] >= 0.0, own_logits + logits_in[...], MASKED)
+    raised = jnp.exp(logits - jnp.max(logits, axis=0, keepdims=True))
+    tables[0, 1] = raised / jnp.sum(raised, axis=0, keepdims=True)
+    table_z = [None] + [send(tables.at[0], tables.at[dz], by_z[dz]) for dz in (1, 2, 3)]
+    table_y = [send(tables.at[0], tables.at[4], by_y)]
+    table_core = {0: send(tables.at[0], tables.at[8], by_core)}
 
     def arrive_z(dz):
+        table_z[dz].wait_recv()
+        table_y.append(send(tables.at[dz], tables.at[4 + dz], by_y))
+        table_core[dz] = send(tables.at[dz], tables.at[8 + dz], by_core)
         z_first[dz].wait_recv()
         y_first.append(gather_y(dz))
         x_first[dz] = gather_x(dz)
@@ -358,6 +365,8 @@
         y_last.append(gather_y_last(dz))
 
     def arrive_y(dz):
+        table_y[dz].wait_recv()
+        table_core[4 + dz] = send(tables.at[4 + dz], tables.at[12 + dz], by_core)
         y_first[dz].wait_recv()
         x_first[4 + dz] = gather_x(4 + dz)
         x_first[dz].wait_recv()
@@ -370,71 +379,61 @@
 
     expert_row = lax.broadcasted_iota(jnp.int32, (experts, count), 0) == place
     slot_row = lax.broadcasted_iota(jnp.int32, (capacity, count), 0)
-
-    def experts_on(dz):
+    units = hidden.shape[1]
+    features = rows_in.shape[1]
+
+    def rows_of(step):
+        return slice(step * capacity, (step + 1) * capacity)
+
+    def hidden_on(dz):
         for step in range(BATCH):
             slot = dz + 4 * step
-            slots = slots_all[slot]
-            halves = [tokens[slot, 0], tokens[slot, 1]]
-            logits = sum(
-                lax.dot_general(
-                    router_ref[:, half * width : (half + 1) * width],
-                    halves[half],
-                    along_last,
-                    preferred_element_type=jnp.float32,
-                )
-                for half in (0, 1)
+            mine, weight = (
+                jnp.sum(jnp.where(expert_row, tables[slot, part], 0.0), axis=0, keepdims=True)
+                for part in (0, 1)
             )
-            logits = jnp.where(slots >= 0.0, logits, MASKED)
-            raised = jnp.exp(logits - jnp.max(logits, axis=0, keepdims=True))
-            share = raised / jnp.sum(raised, axis=0, keepdims=True)
-            weight = jnp.sum(jnp.where(expert_row, share, 0.0), axis=0, keepdims=True)
-            mine = jnp.sum(jnp.where(expert_row, slots, 0.0), axis=0, keepdims=True)
             chosen = slot_row == mine.astype(jnp.int32)
             combine[step] = jnp.where(chosen, weight, 0.0).astype(jnp.bfloat16)
             select = jnp.where(chosen, 1.0, 0.0).astype(jnp.bfloat16)
             for half in (0, 1):
-                rows_in[step * capacity : (step + 1) * capacity, half * width : (half + 1) * width] = (
-                    jnp.dot(select, halves[half], preferred_element_type=jnp.float32).astype(
-                        jnp.bfloat16
-                    )
-                )
-        units = hidden.shape[1]
+                rows_in[rows_of(step), half * width : (half + 1) * width] = jnp.dot(
+                    select, tokens[slot, half], preferred_element_type=jnp.float32
+                ).astype(jnp.bfloat16)
         for start in range(0, units, 256):
             stop = min(start + 256, units)
-            gate_value = lax.dot_general(
-                rows_in[...],
-                gate_up[0, start:stop],
-                along_last,
-                preferred_element_type=jnp.float32,
-            )
-            up_value = lax.dot_general(
-                rows_in[...],
-                gate_up[1, start:stop],
-                along_last,
-                preferred_element_type=jnp.float32,
+            gate_value, up_value = (
+                lax.dot_general(
+                    rows_in[...],
+                    gate_up[part, start:stop],
+                    along_last,
+                    preferred_element_type=jnp.float32,
+                )
+                for part in (0, 1)
             )
             hidden[:, start:stop] = (gate_value / (1.0 + jnp.exp(-gate_value)) * up_value).astype(
                 jnp.bfloat16
             )
-        for half in (0, 1):
-            for start in range(0, width, 512):
-                stop = min(start + 512, width)
-                answered = jnp.dot(
-                    hidden[...],
-                    down[:, half * width + start : half * width + stop],
+
+    def answers_on(dz):
+        for start in range(0, features, 512):
+            stop = min(start + 512, features)
+            rows_in[:, start:stop] = jnp.dot(
+                hidden[...], down[:, start:stop], preferred_element_type=jnp.float32
+            ).astype(jnp.bfloat16)
+        for step in (3, 2, 1, 0):
+            slot = dz + 4 * step
+            for half in (0, 1):
+                partial[slot, half] = lax.dot_general(
+                    combine[step],
+                    rows_in[rows_of(step), half * width : (half + 1) * width],
+                    (((0,), (0,)), ((), ())),
                     preferred_element_type=jnp.float32,
                 ).astype(jnp.bfloat16)
-                for step in range(BATCH):
-                    partial[dz + 4 * step, half, :, start:stop] = lax.dot_general(
-                        combine[step],
-                        answered[step * capacity : (step + 1) * capacity],
-                        (((0,), (0,)), ((), ())),
-                        preferred_element_type=jnp.float32,
-                    ).astype(jnp.bfloat16)
+            if slot >= 8:
+                back_core[slot - 8] = return_core(slot - 8)
 
     def added(one, other):
-        return (one.astype(jnp.float32) + other.astype(jnp.float32)).astype(jnp.bfloat16)
+        return one + other
 
     def return_core(slot):
         return send(partial.at[8 + slot], from_core.at[slot], by_core)
@@ -449,12 +448,11 @@
     back_z = {}
     back_z_last = {}
 
-    def answer(dz):
-        to_core[dz].wait_recv()
-        to_core[4 + dz].wait_recv()
-        experts_on(dz)
-        for slot in (4 + dz, dz):
-            back_core[slot] = return_core(slot)
+    def answer_rows(dz):
+        for slot in (dz, 4 + dz):
+            table_core[slot].wait_recv()
+            to_core[slot].wait_recv()
+        hidden_on(dz)
 
     def core_sum(dz):
         for slot in (4 + dz, dz):
@@ -486,27 +484,29 @@
     arrive_z(1)
     arrive_x(0)
     arrive_y(1)
-    for one in slots_core:
-        one.wait_recv()
     for one in weights:
         one.wait()
-    answer(0)
+    answer_rows(0)
     arrive_z(2)
+    answers_on(0)
     arrive_x(1)
     arrive_y(2)
+    answer_rows(1)
+    arrive_z(3)
+    answers_on(1)
     core_sum(0)
-    answer(1)
-    arrive_z(3)
     arrive_x(2)
     arrive_y(3)
+    answer_rows(2)
     core_sum(1)
     x_sum(0)
-    answer(2)
+    answers_on(2)
     arrive_x(3)
+    answer_rows(3)
     x_sum(1)
     core_sum(2)
+    answers_on(3)
     y_sum(1)
-    answer(3)
     x_sum(2)
     core_sum(3)
     y_sum(2)
@@ -581,7 +581,9 @@
             pltpu.VMEM((count, width), low),
             pltpu.VMEM((8, count), wide),
             pltpu.VMEM((8, count), wide),
-            pltpu.VMEM((16,) + slots.shape, wide),
+            pltpu.VMEM(slots.shape, wide),
+            pltpu.VMEM(slots.shape, wide),
+            pltpu.VMEM((16, 2) + slots.shape, wide),
             pltpu.VMEM((16, 2, count, width), low),
             pltpu.VMEM((16, 2, count, width), low),
             pltpu.VMEM((8, 2, count, width), low),
@@ -597,8 +599,8 @@
             pltpu.VMEM((BATCH * capacity, units), low),
             pltpu.VMEM((BATCH, capacity, count), low),
             pltpu.SemaphoreType.DMA((6,)),
-            pltpu.SemaphoreType.DMA((79,)),
-            pltpu.SemaphoreType.DMA((79,)),
+            pltpu.SemaphoreType.DMA((80,)),
+            pltpu.SemaphoreType.DMA((80,)),
         ],
         compiler_params=pltpu.CompilerParams(
             collective_id=0, has_side_effects=True, vmem_limit_bytes=60 * 1024 * 1024
@@ -656,7 +658,7 @@
         query,
         key_new,
         value_new,
-        norm_gain.reshape(2, 1, width),
+        norm_gain.astype(jnp.float32).reshape(1, 2 * width),
         slot_table(routes, experts_all),
         w_router.T,
         cache_kv,

time: 121 us -> 134 us (1.11)
  the two profiles are of different devices: /device:TPU:8 before, /device:TPU:14 now
where the time goes in v3:
time: 134 us
  Pallas kernels  127 us (95%)
  local copies, waits for them, and re-layouts  3.34 us (2%)
  other arithmetic  1.98 us (1%)
    pallas_call x1, Pallas kernels, layer(): pl.pallas_call(layer_kernel, out_shape=(block, block), in_specs=[pl.Block...  127 us
    unnamed x2, local copies, waits for them, and re-layouts  3.34 us

profile of v3, /device:TPU:14, one launch (start us, length us, event | category | flops | bytes accessed | tf_op | source)
XLA Modules:
  0.0 133.6 jit_solution(3061821943163474058)
XLA Ops:
  0.6 0.7 fusion
  1.3 0.7 convolution_select_fusion.slots_ref
  2.1 1.3 reshape.12
  3.3 126.9 %shard_map.131 = (bf16[128,1024]{1,0:T(8,128)(2,1)}, bf16[128,1024]{1,0:T(8,128)(2,1)}) custom-call(s32[16]{0:T(128)} %length_ref.1, bf16[128,1024]{1,0:T(8,128)(2,1)} %resid_ref.1, bf16[128,1024]{1,0:T(8,128)(2,1)} %query_ref.1, bf16[128,1024]{1,0:T(8,128)(2,1)} %key_ref.1, bf16[128,1024]{1,0:T(8,128)(2,1)} %value_ref.1, f32[1,2048]{1,0:T(1,128)} %bitcast.5, ...), custom_call_target="tpu_custom_call" | custom-call | flops 12000000000 | bytes 18000000 | tf_op jit(solution)/shard_map/pallas_call | solution.py:571
  130.2 1.7 %copy.16 = bf16[128,1024]{1,0:T(8,128)(2,1)} copy(bf16[128,1024]{1,0:T(8,128)(2,1)} %get-tuple-element.4) | data formatting | bytes 524288
  131.9 1.7 %copy.17 = bf16[128,1024]{1,0:T(8,128)(2,1)} copy(bf16[128,1024]{1,0:T(8,128)(2,1)} %get-tuple-element.5) | data formatting | bytes 524288

commit v4 on v3

--- a/solution.py
+++ b/solution.py
@@ -327,42 +327,62 @@
     normed = (after * inverse * gain_ref[:, half_here]).astype(jnp.bfloat16)
     tokens[0, here] = normed
 
-    x_last = send(tokens.at[0, here, last], tokens.at[0, here, last], by_x)
-    y_first = [gather_y(0)]
-    x_first = {0: gather_x(0)}
-    z_first = [None]
-    z_last = [None]
-    y_last = []
-    to_core = {}
-    z_first.append(send(tokens.at[0, here, first], tokens.at[1, here, first], by_z[1]))
     own_logits = lax.dot_general(
         router_ref[:, half_here], normed, along_last, preferred_element_type=jnp.float32
     )
     logits_out[...] = own_logits
     logits_sent = send(logits_out, logits_in, by_x)
-    x_last.wait_recv()
-    for dz in (1, 2, 3):
-        if dz > 1:
-            z_first.append(send(tokens.at[0, here, first], tokens.at[dz, here, first], by_z[dz]))
-        z_last.append(send(tokens.at[0, :, last], tokens.at[dz, :, last], by_z[dz]))
-    y_last.append(gather_y_last(0))
+    x_last = send(tokens.at[0, here, last], tokens.at[0, here, last], by_x)
+    y_first = {0: gather_y(0)}
+    x_first = {0: gather_x(0)}
+    z_first = {}
+    z_last = {}
+    y_last = {}
+    to_core = {}
+
+    def gather_z(dz):
+        z_first[dz] = send(tokens.at[0, here, first], tokens.at[dz, here, first], by_z[dz])
+
+    def gather_z_last(dz):
+        z_last[dz] = send(tokens.at[0, :, last], tokens.at[dz, :, last], by_z[dz])
+
+    gather_z(1)
     logits_sent.wait_recv()
     logits = jnp.where(slots_ref[...] >= 0.0, own_logits + logits_in[...], MASKED)
     raised = jnp.exp(logits - jnp.max(logits, axis=0, keepdims=True))
     tables[0, 1] = raised / jnp.sum(raised, axis=0, keepdims=True)
-    table_z = [None] + [send(tables.at[0], tables.at[dz], by_z[dz]) for dz in (1, 2, 3)]
-    table_y = [send(tables.at[0], tables.at[4], by_y)]
+    table_z = {dz: send(tables.at[0], tables.at[dz], by_z[dz]) for dz in (1, 2, 3)}
+    table_y = {0: send(tables.at[0], tables.at[4], by_y)}
     table_core = {0: send(tables.at[0], tables.at[8], by_core)}
+    x_last.wait_recv()
+    gather_z_last(1)
+    y_last[0] = gather_y_last(0)
+    gather_z(3)
+    gather_z_last(3)
+
+    def pass_first():
+        z_first[3].wait_recv()
+        z_first[2] = send(tokens.at[3, here, first], tokens.at[2, here, first], by_z[1])
+        y_first[3] = gather_y(3)
+        x_first[3] = gather_x(3)
+
+    def pass_last():
+        z_last[3].wait_recv()
+        z_last[2] = send(tokens.at[3, :, last], tokens.at[2, :, last], by_z[1])
+        y_last[3] = gather_y_last(3)
+
+    def pass_tables():
+        for dz in (1, 2, 3):
+            table_z[dz].wait_recv()
+            table_y[dz] = send(tables.at[dz], tables.at[4 + dz], by_y)
+            table_core[dz] = send(tables.at[dz], tables.at[8 + dz], by_core)
 
     def arrive_z(dz):
-        table_z[dz].wait_recv()
-        table_y.append(send(tables.at[dz], tables.at[4 + dz], by_y))
-        table_core[dz] = send(tables.at[dz], tables.at[8 + dz], by_core)
         z_first[dz].wait_recv()
-        y_first.append(gather_y(dz))
+        y_first[dz] = gather_y(dz)
         x_first[dz] = gather_x(dz)
         z_last[dz].wait_recv()
-        y_last.append(gather_y_last(dz))
+        y_last[dz] = gather_y_last(dz)
 
     def arrive_y(dz):
         table_y[dz].wait_recv()
@@ -469,58 +489,72 @@
 
     def y_sum(dz):
         back_y_last[dz].wait_recv()
-        partial[dz, :, FIRST:] = added(partial[dz, :, FIRST:], from_y_last[dz])
-        back_z_last[dz] = send(partial.at[dz, :, last], from_z_last.at[dz - 1], by_z[dz])
+        total = added(partial[dz, :, FIRST:], from_y_last[dz])
+        if dz == 2:
+            back_z_last[3].wait_recv()
+            total = added(total, from_z_last[2])
+        partial[dz, :, FIRST:] = total
+        back_z_last[dz] = send(
+            partial.at[dz, :, last], from_z_last.at[dz - 1], by_z[2 if dz == 2 else 1]
+        )
         back_x[dz].wait_recv()
         back_y[dz].wait_recv()
-        partial[dz, here, :FIRST] = (
+        total = (
             partial[dz, here, :FIRST].astype(jnp.float32)
             + from_x[dz].astype(jnp.float32)
             + from_y[dz].astype(jnp.float32)
-        ).astype(jnp.bfloat16)
-        back_z[dz] = send(partial.at[dz, here, first], from_z.at[dz - 1], by_z[dz])
+        )
+        if dz == 2:
+            back_z[3].wait_recv()
+            total = total + from_z[2].astype(jnp.float32)
+        partial[dz, here, :FIRST] = total.astype(jnp.bfloat16)
+        back_z[dz] = send(
+            partial.at[dz, here, first], from_z.at[dz - 1], by_z[2 if dz == 2 else 1]
+        )
 
     arrive_y(0)
     arrive_z(1)
+    pass_tables()
     arrive_x(0)
     arrive_y(1)
     for one in weights:
         one.wait()
     answer_rows(0)
-    arrive_z(2)
+    pass_first()
     answers_on(0)
     arrive_x(1)
+    core_sum(0)
+    answer_rows(1)
+    pass_last()
+    answers_on(1)
+    arrive_y(3)
+    arrive_z(2)
+    x_sum(0)
+    arrive_x(3)
+    core_sum(1)
     arrive_y(2)
-    answer_rows(1)
-    arrive_z(3)
-    answers_on(1)
-    core_sum(0)
+    answer_rows(3)
+    answers_on(3)
     arrive_x(2)
-    arrive_y(3)
+    x_sum(1)
     answer_rows(2)
-    core_sum(1)
-    x_sum(0)
+    core_sum(3)
     answers_on(2)
-    arrive_x(3)
-    answer_rows(3)
-    x_sum(1)
+    y_sum(1)
+    x_sum(3)
     core_sum(2)
-    answers_on(3)
-    y_sum(1)
+    y_sum(3)
     x_sum(2)
-    core_sum(3)
     y_sum(2)
-    x_sum(3)
-    y_sum(3)
     back_y_last[0].wait_recv()
-    for dz in (1, 2, 3):
+    for dz in (1, 2):
         back_z_last[dz].wait_recv()
 
     def last_sum(half):
         total = partial[0, half, FIRST:].astype(jnp.float32) + from_y_last[0, half].astype(
             jnp.float32
         )
-        for dz in (1, 2, 3):
+        for dz in (1, 2):
             total = total + from_z_last[dz - 1, half].astype(jnp.float32)
         return total
 
@@ -528,14 +562,14 @@
     back_x_last = send(partial.at[0, there, last], from_x_last, by_x)
     back_x[0].wait_recv()
     back_y[0].wait_recv()
-    for dz in (1, 2, 3):
+    for dz in (1, 2):
         back_z[dz].wait_recv()
     total = (
         partial[0, here, :FIRST].astype(jnp.float32)
         + from_x[0].astype(jnp.float32)
         + from_y[0].astype(jnp.float32)
     )
-    for dz in (1, 2, 3):
+    for dz in (1, 2):
         total = total + from_z[dz - 1].astype(jnp.float32)
     out_ref[:FIRST] = total.astype(jnp.bfloat16)
     total = last_sum(here)

time: 134 us -> 119 us (0.89)
  the two profiles are of different devices: /device:TPU:14 before, /device:TPU:0 now
where the time goes in v4:
time: 119 us; the launch traced here: 118 us
  Pallas kernels  112 us (94%)
  local copies, waits for them, and re-layouts  3.34 us (3%)
  other arithmetic  1.98 us (2%)
    pallas_call x1, Pallas kernels, layer(): pl.pallas_call(layer_kernel, out_shape=(block, block), in_specs=[pl.Block...  112 us
    unnamed x2, local copies, waits for them, and re-layouts  3.34 us

profile of v4, /device:TPU:0, one launch (start us, length us, event | category | flops | bytes accessed | tf_op | source)
XLA Modules:
  0.0 118.4 jit_solution(8305842066766616697)
XLA Ops:
  0.6 0.7 fusion
  1.3 0.7 convolution_select_fusion.slots_ref
  2.1 1.3 %reshape.12 = f32[2048]{0:T(1024)} convert(bf16[2048]{0:T(1024)(128)(2,1)} %param.19) | non-fusion elementwise | flops 2048 | bytes 12288 | tf_op jit(solution)/shard_map/reshape | solution.py:695
  3.3 111.7 %shard_map.131 = (bf16[128,1024]{1,0:T(8,128)(2,1)}, bf16[128,1024]{1,0:T(8,128)(2,1)}) custom-call(s32[16]{0:T(128)} %length_ref.1, bf16[128,1024]{1,0:T(8,128)(2,1)} %resid_ref.1, bf16[128,1024]{1,0:T(8,128)(2,1)} %query_ref.1, bf16[128,1024]{1,0:T(8,128)(2,1)} %key_ref.1, bf16[128,1024]{1,0:T(8,128)(2,1)} %value_ref.1, f32[1,2048]{1,0:T(1,128)} %bitcast.5, ...), custom_call_target="tpu_custom_call" | custom-call | flops 12000000000 | bytes 18000000 | tf_op jit(solution)/shard_map/pallas_call | solution.py:605
  115.1 1.7 %copy.16 = bf16[128,1024]{1,0:T(8,128)(2,1)} copy(bf16[128,1024]{1,0:T(8,128)(2,1)} %get-tuple-element.4) | data formatting | bytes 524288
  116.7 1.7 %copy.17 = bf16[128,1024]{1,0:T(8,128)(2,1)} copy(bf16[128,1024]{1,0:T(8,128)(2,1)} %get-tuple-element.5) | data formatting | bytes 524288

commit v5 on v4

--- a/solution.py
+++ b/solution.py
@@ -419,20 +419,15 @@
                 rows_in[rows_of(step), half * width : (half + 1) * width] = jnp.dot(
                     select, tokens[slot, half], preferred_element_type=jnp.float32
                 ).astype(jnp.bfloat16)
-        for start in range(0, units, 256):
-            stop = min(start + 256, units)
-            gate_value, up_value = (
-                lax.dot_general(
-                    rows_in[...],
-                    gate_up[part, start:stop],
-                    along_last,
-                    preferred_element_type=jnp.float32,
-                )
-                for part in (0, 1)
+        gate_value, up_value = (
+            lax.dot_general(
+                gate_up[part], rows_in[...], along_last, preferred_element_type=jnp.float32
             )
-            hidden[:, start:stop] = (gate_value / (1.0 + jnp.exp(-gate_value)) * up_value).astype(
-                jnp.bfloat16
-            )
+            for part in (0, 1)
+        )
+        hidden[...] = jnp.transpose(
+            (gate_value / (1.0 + jnp.exp(-gate_value)) * up_value).astype(jnp.bfloat16)
+        )
 
     def answers_on(dz):
         for start in range(0, features, 512):
@@ -540,9 +535,9 @@
     answer_rows(2)
     core_sum(3)
     answers_on(2)
+    core_sum(2)
     y_sum(1)
     x_sum(3)
-    core_sum(2)
     y_sum(3)
     x_sum(2)
     y_sum(2)

time: 119 us -> 120 us (level)
    pallas_call x1, Pallas kernels: 112 us -> 113 us  [layer(): pl.pallas_call(layer_kernel, out_shape=(block, block), in_specs=[pl.Block...]
where the time goes in v5:
time: 120 us
  Pallas kernels  113 us (94%)
  local copies, waits for them, and re-layouts  3.34 us (3%)
  other arithmetic  1.98 us (2%)
    pallas_call x1, Pallas kernels, layer(): pl.pallas_call(layer_kernel, out_shape=(block, block), in_specs=[pl.Block...  113 us
    unnamed x2, local copies, waits for them, and re-layouts  3.34 us

profile of v5, /device:TPU:0, one launch (start us, length us, event | category | flops | bytes accessed | tf_op | source)
XLA Modules:
  0.0 119.9 jit_solution(14146026901014617008)
XLA Ops:
  0.6 0.7 fusion
  1.3 0.7 convolution_select_fusion.slots_ref
  2.1 1.3 %reshape.12 = f32[2048]{0:T(1024)} convert(bf16[2048]{0:T(1024)(128)(2,1)} %param.19) | non-fusion elementwise | flops 2048 | bytes 12288 | tf_op jit(solution)/shard_map/reshape | solution.py:690
  3.3 113.2 %shard_map.131 = (bf16[128,1024]{1,0:T(8,128)(2,1)}, bf16[128,1024]{1,0:T(8,128)(2,1)}) custom-call(s32[16]{0:T(128)} %length_ref.1, bf16[128,1024]{1,0:T(8,128)(2,1)} %resid_ref.1, bf16[128,1024]{1,0:T(8,128)(2,1)} %query_ref.1, bf16[128,1024]{1,0:T(8,128)(2,1)} %key_ref.1, bf16[128,1024]{1,0:T(8,128)(2,1)} %value_ref.1, f32[1,2048]{1,0:T(1,128)} %bitcast.5, ...), custom_call_target="tpu_custom_call" | custom-call | flops 12000000000 | bytes 18000000 | tf_op jit(solution)/shard_map/pallas_call | solution.py:600
  116.6 1.7 %copy.16 = bf16[128,1024]{1,0:T(8,128)(2,1)} copy(bf16[128,1024]{1,0:T(8,128)(2,1)} %get-tuple-element.4) | data formatting | bytes 524288
  118.2 1.7 %copy.17 = bf16[128,1024]{1,0:T(8,128)(2,1)} copy(bf16[128,1024]{1,0:T(8,128)(2,1)} %get-tuple-element.5) | data formatting | bytes 524288
